TPU v7x, 128 devices: a whole 4x4x4 slice. The times are simulated.
128 devices in a mesh: fsdp: 128 (over z, x, y, core).
Axes of the slice: x: 4, y: 4, z: 4, core: 2. Of those that a mesh axis runs over, the one named last changes fastest.
Arguments:
- tokens: bfloat16 [65536, 768], P('fsdp'), may hold values from -6 to 6
- in_weight: bfloat16 [2574336], P('fsdp'), may hold values from -0.21875 to 0.21875
- out_weight: bfloat16 [1179648], P('fsdp'), may hold values from -0.15625 to 0.15625
- norm_gain: float32 [768], replicated, may hold values from 0.1 to 1.9
- conv_weight: float32 [4, 1792], replicated, may hold values from -3 to 3
- conv_bias: float32 [1792], replicated, may hold values from -3 to 3
- dt_bias: float32 [24], replicated, may hold values from -4.5 to -1
- a_log: float32 [24], replicated, may hold values from 0 to 2.8
- d_skip: float32 [24], replicated, may hold values from 0.5 to 2
- gated_gain: float32 [1536], replicated, may hold values from 0.1 to 1.9
- cotangent: bfloat16 [65536, 768], P('fsdp'), may hold values from -6 to 6
Outputs:
- output: bfloat16 [65536, 768], P('fsdp')
- grad_tokens: float32 [65536, 768], P('fsdp')
- grad_in_weight: float32 [2574336], P('fsdp')
- grad_out_weight: float32 [1179648], P('fsdp')
- grad_norm_gain: float32 [768], replicated
- grad_conv_weight: float32 [4, 1792], replicated
- grad_conv_bias: float32 [1792], replicated
- grad_dt_bias: float32 [24], replicated
- grad_a_log: float32 [24], replicated
- grad_d_skip: float32 [24], replicated
- grad_gated_gain: float32 [1536], replicated
All inputs are finite; a program needn't handle non-finite values.
Results may differ from a plain program's by a relative error of at most 0.0092.
Values may be sent and summed in bfloat16 or wider, within the bound.
No kernel may reach another device: no remote copies, remote signals or barrier semaphores. Data moves between devices by JAX's collectives and lax.ppermute only.
A program may use at most 128 MiB of HBM per device.

v0:
```python
import jax
import jax.numpy as jnp
from jax import lax
from jax.sharding import PartitionSpec as P

D = 768
NH = 24
DS = 128
HEAD = 64
CONV = 4
LEN = 256
DI = 1536
CONV_CH = 1792
NCOL = 3352


epsilon = 1e-05


def silu_slope(value):
    sigma = jax.nn.sigmoid(value)
    return sigma * (1.0 + value * (1.0 - sigma))


def per_device(
    tokens,
    in_weight,
    out_weight,
    norm_gain,
    conv_weight,
    conv_bias,
    dt_bias,
    a_log,
    d_skip,
    gated_gain,
    cotangent,
):
    row_count = tokens.shape[0]
    seq_count = row_count // LEN
    gathered = (
        lax.all_gather(in_weight, "fsdp", axis=0, tiled=True),
        lax.all_gather(out_weight, "fsdp", axis=0, tiled=True),
    )
    input_weight = gathered[0].reshape(D, NCOL)
    output_weight = gathered[1].reshape(DI, D)
    input_rows = tokens.astype(jnp.float32)
    inv_rms = lax.rsqrt(jnp.mean(input_rows * input_rows, axis=-1, keepdims=True) + epsilon)
    normal = input_rows * inv_rms
    hidden_state = (normal * norm_gain).astype(jnp.bfloat16)
    projected_rows = jnp.dot(hidden_state, input_weight, preferred_element_type=jnp.float32)
    gate_in = projected_rows[:, :DI]
    conv_input = projected_rows[:, DI : DI + CONV_CH].reshape(seq_count, LEN, CONV_CH)
    dt_raw = projected_rows[:, DI + CONV_CH :].reshape(seq_count, LEN, NH)
    padded = jnp.pad(conv_input, ((0, 0), (CONV - 1, 0), (0, 0)))
    conv_sum = conv_bias + conv_weight[0] * padded[:, 0:LEN]
    for offset in range(1, CONV):
        conv_sum = conv_sum + conv_weight[offset] * padded[:, offset : offset + LEN]
    activated = jax.nn.silu(conv_sum)
    heads_x = activated[..., :DI].astype(jnp.bfloat16).reshape(seq_count, LEN, NH, HEAD)
    b_state = activated[..., DI : DI + DS].astype(jnp.bfloat16)
    c_state = activated[..., DI + DS :].astype(jnp.bfloat16)
    dt_pre = dt_raw + dt_bias
    dt_step = jax.nn.softplus(dt_pre)
    decay_rate = -jnp.exp(a_log)
    cumulative = jnp.cumsum(dt_step * decay_rate, axis=1)
    scores = jnp.einsum("std,sud->stu", c_state, b_state, preferred_element_type=jnp.float32)
    cum_heads = jnp.swapaxes(cumulative, 1, 2)
    step_heads = jnp.swapaxes(dt_step, 1, 2)
    causal = jnp.arange(LEN)[:, None] >= jnp.arange(LEN)[None, :]
    log_gap = cum_heads[:, :, :, None] - cum_heads[:, :, None, :]
    decay_factor = jnp.where(causal, jnp.exp(jnp.where(causal, log_gap, 0.0)), 0.0)
    mix_weight = (scores[:, None] * decay_factor * step_heads[:, :, None, :]).astype(jnp.bfloat16)
    ssd_out = jnp.einsum("shtu,suhp->sthp", mix_weight, heads_x, preferred_element_type=jnp.float32)
    x_float = heads_x.astype(jnp.float32)
    y_heads = (ssd_out + d_skip[:, None] * x_float).reshape(row_count, DI)
    gate_act = jax.nn.silu(gate_in)
    gated_value = y_heads * gate_act
    gated_inv = lax.rsqrt(jnp.mean(gated_value * gated_value, axis=-1, keepdims=True) + epsilon)
    gnorm = gated_value * gated_inv
    normed_input = (gnorm * gated_gain).astype(jnp.bfloat16)
    mixed_out = jnp.dot(normed_input, output_weight, preferred_element_type=jnp.float32)
    output = (input_rows + mixed_out).astype(jnp.bfloat16)
    again = (
        lax.all_gather(in_weight, "fsdp", axis=0, tiled=True),
        lax.all_gather(out_weight, "fsdp", axis=0, tiled=True),
    )
    input_weight = again[0].reshape(D, NCOL)
    output_weight = again[1].reshape(DI, D)
    cot_float = cotangent.astype(jnp.float32)
    grad_wout = jnp.dot(normed_input.T, cotangent, preferred_element_type=jnp.float32)
    d_normed = jnp.dot(cotangent, output_weight.T, preferred_element_type=jnp.float32)
    grad_gated_gain = jnp.sum(d_normed * gnorm, axis=0)
    d_gn = d_normed * gated_gain
    d_gated = gated_inv * (d_gn - gnorm * jnp.mean(d_gn * gnorm, axis=-1, keepdims=True))
    d_y = d_gated * gate_act
    d_gate = d_gated * y_heads * silu_slope(gate_in)
    d_y_heads = d_y.reshape(seq_count, LEN, NH, HEAD)
    d_ssd = d_y_heads.astype(jnp.bfloat16)
    grad_d_skip = jnp.sum(d_y_heads * x_float, axis=(0, 1, 3))
    d_x = d_skip[:, None] * d_y_heads + jnp.einsum(
        "shtu,sthp->suhp", mix_weight, d_ssd, preferred_element_type=jnp.float32
    )
    d_mix = jnp.einsum("sthp,suhp->shtu", d_ssd, heads_x, preferred_element_type=jnp.float32)
    d_scores = jnp.sum(d_mix * decay_factor * step_heads[:, :, None, :], axis=1).astype(
        jnp.bfloat16
    )
    scored_decay = d_mix * scores[:, None] * decay_factor
    d_gap = scored_decay * step_heads[:, :, None, :]
    d_cum = jnp.swapaxes(jnp.sum(d_gap, axis=-1) - jnp.sum(d_gap, axis=-2), 1, 2)
    d_inc = jnp.flip(jnp.cumsum(jnp.flip(d_cum, 1), axis=1), 1)
    d_step = jnp.swapaxes(jnp.sum(scored_decay, axis=-2), 1, 2) + d_inc * decay_rate
    grad_a_log = jnp.sum(d_inc * dt_step, axis=(0, 1)) * decay_rate
    d_pre = d_step * jax.nn.sigmoid(dt_pre)
    grad_dt_bias = jnp.sum(d_pre, axis=(0, 1))
    d_c = jnp.einsum("stu,sud->std", d_scores, b_state, preferred_element_type=jnp.float32)
    d_b = jnp.einsum("stu,std->sud", d_scores, c_state, preferred_element_type=jnp.float32)
    d_act = jnp.concatenate([d_x.reshape(seq_count, LEN, DI), d_b, d_c], axis=-1)
    d_conv = d_act * silu_slope(conv_sum)
    grad_conv_bias = jnp.sum(d_conv, axis=(0, 1))
    grad_conv_weight = jnp.stack(
        [jnp.sum(d_conv * padded[:, offset : offset + LEN], axis=(0, 1)) for offset in range(CONV)]
    )
    d_padded = jnp.pad(d_conv, ((0, 0), (0, CONV - 1), (0, 0)))
    d_conv_in = conv_weight[0] * d_padded[:, CONV - 1 : CONV - 1 + LEN]
    for offset in range(1, CONV):
        begin = CONV - 1 - offset
        d_conv_in = d_conv_in + conv_weight[offset] * d_padded[:, begin : begin + LEN]
    d_proj = jnp.concatenate(
        [d_gate, d_conv_in.reshape(row_count, CONV_CH), d_pre.reshape(row_count, NH)], axis=-1
    ).astype(jnp.bfloat16)
    grad_win = jnp.dot(hidden_state.T, d_proj, preferred_element_type=jnp.float32)
    grad_in_weight, grad_out_weight = (
        lax.psum_scatter(grad_win.reshape(-1), "fsdp", scatter_dimension=0, tiled=True),
        lax.psum_scatter(grad_wout.reshape(-1), "fsdp", scatter_dimension=0, tiled=True),
    )
    d_hidden = jnp.dot(d_proj, input_weight.T, preferred_element_type=jnp.float32)
    grad_norm_gain = jnp.sum(d_hidden * normal, axis=0)
    d_normal = d_hidden * norm_gain
    grad_tokens = cot_float + inv_rms * (
        d_normal - normal * jnp.mean(d_normal * normal, axis=-1, keepdims=True)
    )
    summed = lax.psum(
        (
            grad_norm_gain,
            grad_conv_weight,
            grad_conv_bias,
            grad_dt_bias,
            grad_a_log,
            grad_d_skip,
            grad_gated_gain,
        ),
        "fsdp",
    )
    return (
        output,
        grad_tokens,
        grad_in_weight,
        grad_out_weight,
        summed[0],
        summed[1],
        summed[2],
        summed[3],
        summed[4],
        summed[5],
        summed[6],
    )


def solution(mesh):
    placed = (
        P("fsdp", None),
        P("fsdp"),
        P("fsdp"),
        P(),
        P(),
        P(),
        P(),
        P(),
        P(),
        P(),
        P("fsdp", None),
    )
    return jax.shard_map(
        per_device,
        mesh=mesh,
        in_specs=placed,
        out_specs=(
            P("fsdp", None),
            P("fsdp", None),
            P("fsdp"),
            P("fsdp"),
            P(),
            P(),
            P(),
            P(),
            P(),
            P(),
            P(),
        ),
        check_vma=False,
    )
```

profile of v0, /device:TPU:1, one launch (start us, length us, event | category | flops | bytes accessed | tf_op | source)
XLA Modules:
  0.0 516.1 jit_solution(2594464748093182153)
XLA Ops:
  14.0 158.5 %all-reduce.10.cloned.1.call-done = bf16[2574336]{0:T(1024)(128)(2,1)} async-done(((bf16[2574336]{0:T(1024)(128)(2,1)}), bf16[2574336]{0:T(1024)(128)(2,1)}) %all-reduce.10.cloned.1.call-update) | async-done | bytes 5148688
  172.5 10.5 %reshape.143 = bf16[768,3352]{1,0:T(8,128)(2,1)} reshape(bf16[2574336]{0:T(1024)(128)(2,1)} %all-reduce.10.cloned.1.call-done) | data formatting | bytes 10297344 | tf_op jit(solution)/shard_map/reshape | solution.py:44
  183.0 5.7 %fusion.23 = f32[512,3352]{0,1:T(8,128)S(1)} fusion(bf16[768,3352]{1,0:T(8,128)(2,1)} %reshape.143, bf16[512,768]{1,0:T(8,128)(2,1)S(1)} %copy-done.4, f32[768]{0:T(1024)S(1)} %copy-done.12, f32[512]{0:T(512)S(1)} %add_rsqrt_fusion.1), kind=kOutput, calls=%fused_computation.57 | convolution fusion | flops 2637692928 | bytes 12805120 | tf_op jit(solution)/shard_map/dot_general | solution.py:50
  192.7 5.2 %copy.144 = f32[512,1792]{1,0:T(8,128)} copy(f32[512,1792]{0,1:T(8,128)} %slice.93) | data formatting | bytes 7340032 | tf_op jit(solution)/shard_map/reshape | solution.py:52
  197.9 8.6 %multiply_convert_fusion.3 = (bf16[2,256,1792]{2,1,0:T(8,128)(2,1)S(1)}, f32[2,256,1792]{2,1,0:T(8,128)}) fusion(f32[2,256,1792]{2,1,0:T(8,128)} %bitcast.77, f32[1792]{0:T(1024)S(1)} %get-tuple-element.29, f32[1792]{0:T(1024)S(1)} %get-tuple-element.30, f32[1792]{0:T(1024)S(1)} %get-tuple-element.28, f32[1792]{0:T(1024)S(1)} %get-tuple-element.27, ...), kind=kLoop, calls=%fused_computation.16 | loop fusion | flops 11927552 | bytes 9210880 | tf_op jit(solution)/shard_map/convert.8
  213.2 5.6 %bitcast_add_fusion.1 = f32[2,256,24,64]{1,3,2,0:T(8,128)S(1)} fusion(bf16[2,256,24,64]{1,3,2,0:T(8,128)(2,1)} %bitcast.85, f32[2,24,256]{2,1,0:T(8,128)} %get-tuple-element.52, f32[2,24,256]{2,1,0:T(8,128)S(1)} %copy_bitcast_fusion, f32[2,256,256]{2,1,0:T(8,128)S(1)} %fusion.30, pred[256,256]{1,0:T(8,128)(4,1)} %iota_compare_fusion, f32[24]{0:T(128)S(1)} %copy-done.43), kind=kOutput, calls=%fused_computation.23 | convolution fusion | flops 423886848 | bytes 5406816 | tf_op jit(solution)/shard_map/shtu,suhp->sthp/dot_general | solution.py:73
  225.5 3.7 copy.143
  229.2 4.0 multiply_reduce_fusion.10
  233.2 3.7 fusion.41
  236.9 5.7 %reshape.158 = f32[1179648]{0:T(1024)} reshape(f32[1536,768]{1,0:T(8,128)} %fusion.41) | data formatting | bytes 9437184 | tf_op jit(solution)/shard_map/reshape | solution.py:134
  242.6 5.3 %reshape.150 = bf16[1536,768]{1,0:T(8,128)(2,1)} reshape(bf16[1179648]{0:T(1024)(128)(2,1)} %all-gather.2.cloned.1.call-done) | data formatting | bytes 4718592 | tf_op jit(solution)/shard_map/reshape | solution.py:45
  248.0 4.6 multiply_reduce_fusion.7
  252.6 6.2 %multiply_reduce_fusion.8 = (f32[1536]{0:T(1024)}, f32[512,1536]{0,1:T(8,128)}, bf16[512,1536]{0,1:T(8,128)(2,1)}) fusion(f32[512,1536]{0,1:T(8,128)S(1)} %copy-done.2, f32[512,3352]{0,1:T(8,128)} %copy-done.1, f32[512]{0:T(512)S(1)} %broadcast_multiply_fusion, f32[512,1536]{0,1:T(8,128)S(1)} %get-tuple-element.46, f32[512,1536]{0,1:T(8,128)S(1)} %get-tuple-element.53, ...), kind=kLoop, calls=%fused_computation.25 | loop fusion | flops 14940672 | bytes 20463616 | tf_op jit(solution)/shard_map/reduce_sum | solution.py:99
  258.8 5.2 %reshape.151 = f32[2,256,24,64]{1,0,3,2:T(2,128)} reshape(f32[512,1536]{0,1:T(8,128)} %get-tuple-element.41) | data formatting | bytes 6291456 | tf_op jit(solution)/shard_map/reshape | solution.py:97
  264.0 10.5 %multiply_reduce_fusion.1 = (f32[2,24,256]{2,1,0:T(8,128)S(1)}, f32[2,24,256]{2,1,0:T(8,128)S(1)}, f32[2,24,256]{2,1,0:T(8,128)}, bf16[2,256,256]{2,1,0:T(8,128)(2,1)S(1)}) fusion(f32[2,24,256]{2,1,0:T(8,128)S(1)} %copy-done.25, f32[2,24,256]{2,1,0:T(8,128)S(1)} %copy-done.24, pred[256,256]{1,0:T(8,128)(4,1)S(1)} %copy-done.21, ...), kind=kOutput, calls=%fused_computation.4 | convolution fusion | flops 440233984 | bytes 5816320 | tf_op jit(solution)/shard_map/sthp,suhp->shtu/dot_general | solution.py:103
  277.5 5.4 %bitcast_add_fusion = f32[2,256,24,64]{1,3,2,0:T(8,128)} fusion(f32[2,256,24,64]{1,0,3,2:T(2,128)S(1)} %copy-done.7, f32[2,24,256]{2,1,0:T(8,128)S(1)} %copy-done.26, f32[2,24,256]{2,1,0:T(8,128)S(1)} %copy-done.24, f32[2,256,256]{2,1,0:T(8,128)S(1)} %copy-done.10, pred[256,256]{1,0:T(8,128)(4,1)S(1)} %copy-done.22, f32[24]{0:T(128)S(1)} %copy-done.43), kind=kOutput, calls=%fused_computation.22 | convolution fusion | flops 423886848 | bytes 6979680 | tf_op jit(solution)/shard_map/shtu,sthp->suhp/dot_general | solution.py:100
  292.2 3.8 copy.124
  296.0 10.7 %fusion.42 = (f32[1792]{0:T(1024)}, f32[1792]{0:T(1024)}, f32[1792]{0:T(1024)}, f32[1792]{0:T(1024)}, f32[1792]{0:T(1024)}, /*index=5*/f32[2,256,1792]{2,1,0:T(8,128)S(1)}) fusion(f32[512,1792]{1,0:T(8,128)} %copy.144, f32[2,256,1792]{2,1,0:T(8,128)} %bitcast.78, f32[2,256,1792]{2,1,0:T(8,128)} %get-tuple-element.48, f32[2,256,128]{2,1,0:T(8,128)S(1)} %fusion.25, ...), kind=kLoop, calls=%fused_computation.99 | loop fusion | flops 17423616 | bytes 18385920 | tf_op jit(solution)/shard_map/reduce_sum | solution.py:119
  311.8 9.4 %fusion.18 = f32[768,3352]{1,0:T(8,128)} fusion(bf16[512,24]{1,0:T(8,128)(2,1)S(1)} %bitcast.87, bf16[512,1792]{1,0:T(8,128)(2,1)} %bitcast.82, bf16[512,1536]{1,0:T(8,128)(2,1)} %copy.130, bf16[512,768]{1,0:T(8,128)(2,1)} %param.11, f32[768]{0:T(1024)S(1)} %copy-done.12, f32[512]{0:T(512)S(1)} %add_rsqrt_fusion.1), kind=kOutput, calls=%fused_computation.52 | convolution fusion | flops 2647990272 | bytes 14521344 | tf_op jit(solution)/shard_map/dot_general | solution.py:131
  321.2 11.5 %reshape.157 = f32[2574336]{0:T(1024)} reshape(f32[768,3352]{1,0:T(8,128)} %fusion.18) | data formatting | bytes 20594688 | tf_op jit(solution)/shard_map/reshape | solution.py:133
  333.8 8.0 %fusion.14 = (f32[768]{0:T(1024)S(1)}, f32[512]{0:T(512)S(1)}, f32[512,768]{1,0:T(8,128)}) fusion(bf16[512,768]{1,0:T(8,128)(2,1)} %param.11, f32[512]{0:T(512)S(1)} %add_rsqrt_fusion.1, f32[768]{0:T(1024)S(1)} %copy-done.12, bf16[768,3352]{1,0:T(8,128)(2,1)} %reshape.143, bf16[512,24]{1,0:T(8,128)(2,1)S(1)} %bitcast.88, bf16[512,1792]{1,0:T(8,128)(2,1)} %bitcast.83, ...), kind=kOutput, calls=%fused_computation.47 | convolution fusion | flops 2649168640 | bytes 10950656 | tf_op jit(solution)/shard_map/dot_general | solution.py:136
  341.8 65.7 %all-reduce.5 = (f32[768]{0:T(1024)}, f32[4,1792]{1,0:T(4,128)}, f32[1792]{0:T(1024)}, f32[24]{0:T(128)}, f32[24]{0:T(128)}, /*index=5*/f32[24]{0:T(128)}, f32[1536]{0:T(1024)}) all-reduce(f32[768]{0:T(1024)S(1)} %get-tuple-element.25, f32[4,1792]{1,0:T(4,128)S(1)} %pad_maximum_fusion.3, ...), channel_id=1, replica_groups=mesh['fsdp'=128] {'fsdp'}, use_global_device_ids=true, to_apply=%region_15.16 | all-reduce | flops 11336 | bytes 90688 | tf_op jit(solution)/shard_map/psum | solution.py:142
  407.5 3.6 fusion.13
  413.7 92.4 %all-reduce.12.cloned.1.call-done = (f32[2574336]{0:T(1024)}, f32[1179648]{0:T(1024)}) async-done(((f32[2574336]{0:T(1024)}, f32[1179648]{0:T(1024)}), (f32[2574336]{0:T(1024)}, f32[1179648]{0:T(1024)})) %all-reduce.12.cloned.1.call-update) | async-done | bytes 15015952
  (150 shorter events, 48.1 us)
Async XLA Ops:
  7.2 165.3 %all-reduce.10.cloned.1.call-start = ((), (), s32[]{:S(2)}) async-start(), calls=%async_computation.1 | async-start | bytes 10297344
  11.7 230.9 %all-gather.2.cloned.1.call-start = ((), (), s32[]{:S(2)}) async-start(), calls=%async_computation | async-start | bytes 2377728 | tf_op jit(solution)/shard_map/all_gather | solution.py:42
  12.4 493.7 %all-reduce.12.cloned.1.call-start = ((), (), s32[]{:S(2)}) async-start(), calls=%async_computation.2 | async-start | bytes 30031872
  13.5 184.4 %copy-start.13 = (f32[1792]{0:T(1024)}, f32[1792]{0:T(1024)S(1)}, u32[]{:S(2)}) copy-start(f32[1792]{0:T(1024)S(1)} %get-tuple-element.27) | copy-start | bytes 21508
  13.5 184.4 %copy-start.15 = (f32[1792]{0:T(1024)}, f32[1792]{0:T(1024)S(1)}, u32[]{:S(2)}) copy-start(f32[1792]{0:T(1024)S(1)} %get-tuple-element.28) | copy-start | bytes 21508
  13.5 184.4 %copy-start.17 = (f32[1792]{0:T(1024)}, f32[1792]{0:T(1024)S(1)}, u32[]{:S(2)}) copy-start(f32[1792]{0:T(1024)S(1)} %get-tuple-element.29) | copy-start | bytes 21508
  13.5 184.4 %copy-start.19 = (f32[1792]{0:T(1024)}, f32[1792]{0:T(1024)S(1)}, u32[]{:S(2)}) copy-start(f32[1792]{0:T(1024)S(1)} %get-tuple-element.30) | copy-start | bytes 21508
  14.0 168.9 %copy-start.12 = (f32[768]{0:T(1024)S(1)}, f32[768]{0:T(1024)}, u32[]{:S(2)}) copy-start(f32[768]{0:T(1024)} %param.14) | copy-start | bytes 9220
  192.7 5.2 %copy-start.38 = (f32[1792]{0:T(1024)S(1)}, f32[1792]{0:T(1024)}, u32[]{:S(2)}) copy-start(f32[1792]{0:T(1024)} %param.16) | copy-start | bytes 21508
  206.5 5.6 %copy-start.3 = (bf16[2,256,1792]{2,1,0:T(8,128)(2,1)}, bf16[2,256,1792]{2,1,0:T(8,128)(2,1)S(1)}, u32[]{:S(2)}) copy-start(bf16[2,256,1792]{2,1,0:T(8,128)(2,1)S(1)} %get-tuple-element.47) | copy-start | bytes 5505028
  206.5 6.7 %copy-start.43 = (f32[24]{0:T(128)S(1)}, f32[24]{0:T(128)}, u32[]{:S(2)}) copy-start(f32[24]{0:T(128)} %param.19) | copy-start | bytes 292
  233.2 19.4 %copy-start.29 = (f32[512]{0:T(512)}, f32[512]{0:T(512)S(1)}, u32[]{:S(2)}) copy-start(f32[512]{0:T(512)S(1)} %add_rsqrt_fusion) | copy-start | bytes 6148
  264.0 13.5 %copy-start.7 = (f32[2,256,24,64]{1,0,3,2:T(2,128)S(1)}, f32[2,256,24,64]{1,0,3,2:T(2,128)}, u32[]{:S(2)}) copy-start(f32[2,256,24,64]{1,0,3,2:T(2,128)} %reshape.151) | copy-start | bytes 9437188
  264.0 13.5 %copy-start.10 = (f32[2,256,256]{2,1,0:T(8,128)S(1)}, f32[2,256,256]{2,1,0:T(8,128)}, u32[]{:S(2)}) copy-start(f32[2,256,256]{2,1,0:T(8,128)} %copy-done.9) | copy-start | bytes 1572868
  264.0 13.5 %copy-start.22 = (pred[256,256]{1,0:T(8,128)(4,1)S(1)}, pred[256,256]{1,0:T(8,128)(4,1)}, u32[]{:S(2)}) copy-start(pred[256,256]{1,0:T(8,128)(4,1)} %iota_compare_fusion) | copy-start | bytes 196612
  264.0 13.5 %copy-start.26 = (f32[2,24,256]{2,1,0:T(8,128)S(1)}, f32[2,24,256]{2,1,0:T(8,128)}, u32[]{:S(2)}) copy-start(f32[2,24,256]{2,1,0:T(8,128)} %get-tuple-element.52) | copy-start | bytes 147460
  295.9 10.7 %copy-start.14 = (f32[1792]{0:T(1024)S(1)}, f32[1792]{0:T(1024)}, u32[]{:S(2)}) copy-start(f32[1792]{0:T(1024)} %copy-done.13) | copy-start | bytes 21508
  295.9 10.7 %copy-start.16 = (f32[1792]{0:T(1024)S(1)}, f32[1792]{0:T(1024)}, u32[]{:S(2)}) copy-start(f32[1792]{0:T(1024)} %copy-done.15) | copy-start | bytes 21508
  295.9 10.7 %copy-start.18 = (f32[1792]{0:T(1024)S(1)}, f32[1792]{0:T(1024)}, u32[]{:S(2)}) copy-start(f32[1792]{0:T(1024)} %copy-done.17) | copy-start | bytes 21508
  295.9 10.7 %copy-start.20 = (f32[1792]{0:T(1024)S(1)}, f32[1792]{0:T(1024)}, u32[]{:S(2)}) copy-start(f32[1792]{0:T(1024)} %copy-done.19) | copy-start | bytes 21508
  333.8 8.0 %copy-start.31 = (f32[1792]{0:T(1024)S(1)}, f32[1792]{0:T(1024)}, u32[]{:S(2)}) copy-start(f32[1792]{0:T(1024)} %get-tuple-element.20) | copy-start | bytes 21508
  333.8 8.0 %copy-start.37 = (f32[1536]{0:T(1024)S(1)}, f32[1536]{0:T(1024)}, u32[]{:S(2)}) copy-start(f32[1536]{0:T(1024)} %get-tuple-element.18) | copy-start | bytes 18436
  333.8 8.0 %copy-start.41 = (f32[24]{0:T(128)S(1)}, f32[24]{0:T(128)}, u32[]{:S(2)}) copy-start(f32[24]{0:T(128)} %get-tuple-element.42) | copy-start | bytes 292
  341.8 69.3 %copy-start.30 = (f32[512]{0:T(512)S(1)}, f32[512]{0:T(512)}, u32[]{:S(2)}) copy-start(f32[512]{0:T(512)} %copy-done.29) | copy-start | bytes 6148
  (25 other events, 67.4 us)
Sparse Core Ops, SparseCore 0:
  13.0 159.4 all-reduce.9
  175.4 64.0 all-gather.1
  332.9 173.1 all-reduce.11
where the time goes:
time: 526 us; the launch traced here: 516 us
  waiting for transfers between devices  252 us (48%)
  local copies, waits for them, and re-layouts  77 us (15%)
  blocking collectives  65.7 us (12%)
  matrix products  58.6 us (11%)
  other arithmetic  48.4 us (9%)
  between operations  14.7 us (3%)
    unnamed x5, waiting for transfers between devices  252 us
    psum x1, blocking collectives, per_device(): lax.psum((grad_norm_gain, grad_conv_weight, grad_conv_bias, grad_dt_bias,...  65.7 us
    another operation x8, other arithmetic  16.6 us
    unnamed x97, local copies, waits for them, and re-layouts  12.5 us
    reshape x1, local copies, waits for them, and re-layouts, per_device(): grad_win.reshape(-1)  11.5 us
    reduce_sum x1, other arithmetic, per_device(): grad_conv_bias = jnp.sum(d_conv, axis=(0, 1))  10.7 us
  transfers between devices with their start and end apart: 3, of which 2 were waited for; matrix products, arithmetic and copies ran while one was open for 16% of the time, Pallas kernels for 0%

commit v1 on v0

v1 whole, which is shorter than its diff:
```python
import jax
import jax.numpy as jnp
from jax import lax
from jax.experimental import pallas as pl
from jax.experimental.pallas import tpu as pltpu
from jax.sharding import PartitionSpec as P

D = 768
NH = 24
DS = 128
HEAD = 64
CONV = 4
LEN = 256
DI = 1536
CONV_CH = 1792
NCOL = 3352
ROWS = 512
SEQS = 2
PADLEN = LEN + 8
HALF1 = 1024
WIDE1 = 2048
EPS = 1e-5
LOG2E = 1.4426950408889634
LIMIT = 58 * 1024 * 1024
F32 = jnp.float32
BF16 = jnp.bfloat16
HIGHEST = lax.Precision.HIGHEST


def index_of(z, x, y, c):
    return ((z % 4 * 4 + x % 4) * 4 + y % 4) * 2 + c


def everyone():
    for z in range(4):
        for x in range(4):
            for y in range(4):
                for c in range(2):
                    yield z, x, y, c


def ring_pairs(shift, last):
    pairs = []
    for z, x, y, c in everyone():
        along_z = (c == 0) == last
        to = (z + shift, x, y, c) if along_z else (z, x + shift, y, c)
        pairs.append((index_of(z, x, y, c), index_of(*to)))
    return pairs


CORE_PAIRS = [(index_of(*p), index_of(*p[:3], 1 - p[3])) for p in everyone()]
EIGHTS = [[(z * 4 + x) * 8 + k for k in range(8)] for z in range(4) for x in range(4)]


def ring_gather(value, last):
    return [value] + [
        lax.ppermute(value, "fsdp", ring_pairs(shift, last)) for shift in (1, 2, 3)
    ]


def ring_reduce(parts, last):
    got = [parts[0].astype(F32)] + [
        lax.ppermute(parts[r].astype(BF16), "fsdp", ring_pairs(r, last)).astype(F32)
        for r in (1, 2, 3)
    ]
    return (got[0] + got[2]) + (got[1] + got[3])


def swap_core(value):
    return lax.ppermute(value, "fsdp", CORE_PAIRS)


def dot_nn(a, b):
    return jnp.dot(a, b, preferred_element_type=F32)


def dot_nt(a, b):
    return lax.dot_general(a, b, (((1,), (1,)), ((), ())), preferred_element_type=F32)


def dot_tn(a, b):
    return lax.dot_general(a, b, (((0,), (0,)), ((), ())), preferred_element_type=F32)


def dot_exact(a, b):
    return jnp.dot(a, b, preferred_element_type=F32, precision=HIGHEST)


def sigmoid(v):
    return 0.5 * jnp.tanh(0.5 * v) + 0.5


def softplus(v):
    e = jnp.exp(-jnp.abs(v))
    small = e * (1.0 - e * (0.5 - e * (1.0 / 3.0)))
    return jnp.maximum(v, 0.0) + jnp.where(e < 1e-3, small, jnp.log(1.0 + e))


def iota(shape, dim):
    return lax.broadcasted_iota(jnp.int32, shape, dim)


def source_zx(half, z0, x0, r3, r2):
    zr = jnp.where(half == 0, r3, r2)
    xr = jnp.where(half == 0, r2, r3)
    return lax.rem(z0 - zr + 4, 4) * 4 + lax.rem(x0 - xr + 4, 4)


def slot_of(half, z0, x0, zx):
    dz = lax.rem(zx // 4 - z0 + 4, 4)
    dx = lax.rem(zx % 4 - x0 + 4, 4)
    return jnp.where(half == 0, dz * 4 + dx, dx * 4 + dz)


def head_masks():
    lane = iota((1, 128), 1)
    first = jnp.where(lane < 64, 1.0, 0.0).astype(BF16)
    second = jnp.where(lane < 64, 0.0, 1.0).astype(BF16)
    return first, second


def kernel_a(
    pos, tokens, gain, conv_w, conv_b, dt_bias, rate, d_skip,
    b0, b1, b2, b3, q0, q1, q2, q3,
    hidden, w1, conv_in, slope, xs, bc, dt_pre, acum, bcum, y,
    score, bcum_t, sems,
):
    z0, x0, core = pos[0], pos[1], pos[2]
    copies = []
    for side, refs in enumerate(((b0, b1, b2, b3), (q0, q1, q2, q3))):
        half = core if side == 0 else 1 - core
        col = pl.multiple_of(half * HALF1, HALF1)
        for r3 in range(4):
            for r2 in range(4):
                row = pl.multiple_of(source_zx(half, z0, x0, r3, r2) * 48, 16)
                copies.append(
                    pltpu.make_async_copy(
                        refs[r3].at[pl.ds(r2 * 48, 48)],
                        w1.at[pl.ds(row, 48), pl.ds(col, HALF1)],
                        sems.at[side, r3, r2],
                    )
                )
    for copy in copies:
        copy.start()

    @pl.loop(0, ROWS // 64)
    def _(i):
        rows = pl.ds(pl.multiple_of(i * 64, 64), 64)
        t = tokens[rows].astype(F32)
        inv = lax.rsqrt(jnp.mean(t * t, axis=1, keepdims=True) + EPS)
        hidden[rows] = (t * inv * gain[...]).astype(BF16)

    for s in range(SEQS):
        conv_in[s, 0:8] = jnp.zeros((8, CONV_CH), F32)
    for copy in copies:
        copy.wait()

    def conv_tile(cols, emit):
        p = dot_nn(hidden[...], w1[:, cols])
        for s in range(SEQS):
            conv_in[s, 8:PADLEN, cols] = p[s * LEN : (s + 1) * LEN]
        w = conv_w[:, cols]
        bias = conv_b[:, cols]
        for s in range(SEQS):

            @pl.loop(0, LEN // 32)
            def _(i):
                base = pl.multiple_of(i * 32, 32)
                near = conv_in[s, pl.ds(base, 40), cols]
                total = bias + w[0:1] * near[5:37]
                for k in range(1, CONV):
                    total = total + w[k : k + 1] * near[5 + k : 37 + k]
                sig = sigmoid(total)
                act = total * sig
                rows = pl.ds(pl.multiple_of(s * LEN + base, 32), 32)
                slope[rows, cols] = sig * (1.0 + total * (1.0 - sig))
                emit(rows, act.astype(BF16))

    @pl.loop(0, 6)
    def _(j):
        cols = pl.ds(pl.multiple_of(j * 256, 256), 256)

        def emit(rows, act):
            xs[rows, cols] = act

        conv_tile(cols, emit)

    def emit_bc(rows, act):
        bc[rows] = act

    conv_tile(pl.ds(1536, 256), emit_bc)

    pre = dot_nn(hidden[...], w1[:, CONV_CH : CONV_CH + 128]) + dt_bias[...]
    dt_pre[...] = pre
    step = softplus(pre)
    inc = step * rate[...] * LOG2E
    log_step = jnp.log(jnp.maximum(step, 1e-37)) * LOG2E
    below = iota((LEN, LEN), 0) >= iota((LEN, LEN), 1)
    lower = jnp.where(below, 1.0, 0.0)
    mask0, mask1 = head_masks()
    for s in range(SEQS):
        rows = slice(s * LEN, (s + 1) * LEN)
        a = dot_exact(lower, inc[rows])
        b = a - log_step[rows]
        acum[rows] = a
        bcum[rows] = b
        bcum_t[...] = b.T
        score[...] = jnp.where(below, dot_nt(bc[rows, DS:], bc[rows, :DS]), 0.0)

        @pl.loop(0, NH // 2)
        def _(p):
            lanes = pl.ds(pl.multiple_of(p * 128, 128), 128)
            x = xs[s * LEN : (s + 1) * LEN, lanes]
            turned = pltpu.roll(a, lax.rem(128 - 2 * p, 128), 1)
            top = jnp.zeros((128, 128), F32)
            low = jnp.zeros((128, 128), F32)
            for i, mask in enumerate((mask0, mask1)):
                col = turned[:, i : i + 1]
                row = bcum_t[pl.ds(2 * p + i, 1), :]
                xm = x * mask
                e0 = jnp.exp2(jnp.minimum(col[:128] - row[:, :128], 64.0))
                m0 = (e0 * score[:128, :128]).astype(BF16)
                top = top + dot_nn(m0, xm[:128])
                e1 = jnp.exp2(jnp.minimum(col[128:] - row, 64.0))
                m1 = (e1 * score[128:, :]).astype(BF16)
                low = low + dot_nn(m1, xm)
            skip = d_skip[:, lanes]
            y[s * LEN : s * LEN + 128, lanes] = top + skip * x[:128].astype(F32)
            y[s * LEN + 128 : (s + 1) * LEN, lanes] = low + skip * x[128:].astype(F32)


def kernel_b(
    pos, hidden, y, tokens, cot, gain,
    b0, b1, b2, b3, q0, q1, q2, q3,
    out, d_y, grads, d_hid, gain_grad,
    weights, gate_in, d_normed, normed, d_gate, gate_inv, acc, sems,
):
    z0, x0, core = pos[0], pos[1], pos[2]
    copies = []
    for side, refs in enumerate(((b0, b1, b2, b3), (q0, q1, q2, q3))):
        half = core if side == 0 else 1 - core
        for r3 in range(4):
            for r2 in range(4):
                zx = source_zx(half, z0, x0, r3, r2)
                for lr in range(2):
                    row = jnp.where(half == 0, lr * D + zx * 48, DI + zx * 96 + lr * 48)
                    copies.append(
                        pltpu.make_async_copy(
                            refs[r3].at[pl.ds(r2 * 96 + lr * 48, 48)],
                            weights.at[pl.ds(pl.multiple_of(row, 16), 48)],
                            sems.at[side, r3, r2, lr],
                        )
                    )
    for copy in copies:
        copy.start()
    for copy in copies:
        copy.wait()

    @pl.loop(0, 3)
    def _(j):
        cols = pl.ds(pl.multiple_of(j * 256, 256), 256)
        right = pl.ds(pl.multiple_of(j * 256 + D, 256), 256)
        gate_in[:, cols] = dot_nn(hidden[...], weights[0:D, cols])
        gate_in[:, right] = dot_nn(hidden[...], weights[D:DI, cols])

    @pl.loop(0, ROWS // 16)
    def _(i):
        rows = pl.ds(pl.multiple_of(i * 16, 16), 16)
        g = gate_in[rows]
        gated = y[rows] * (g * sigmoid(g))
        inv = lax.rsqrt(jnp.mean(gated * gated, axis=1, keepdims=True) + EPS)
        gate_inv[rows] = jnp.broadcast_to(inv, (16, 128))
        normed[rows] = (gated * inv * gain[...]).astype(BF16)

    @pl.loop(0, 3)
    def _(j):
        cols = pl.ds(pl.multiple_of(j * 256, 256), 256)
        mixed = dot_nn(normed[...], weights[DI:, cols])
        out[:, cols] = (tokens[:, cols].astype(F32) + mixed).astype(BF16)

    @pl.loop(0, 6)
    def _(j):
        cols = pl.ds(pl.multiple_of(j * 256, 256), 256)
        d_normed[:, cols] = dot_nt(cot[...], weights[pl.ds(pl.multiple_of(j * 256 + DI, 256), 256)])

    acc[...] = jnp.zeros_like(acc)

    @pl.loop(0, ROWS // 16)
    def _(i):
        rows = pl.ds(pl.multiple_of(i * 16, 16), 16)
        g = gate_in[rows]
        sig = sigmoid(g)
        act = g * sig
        yv = y[rows]
        inv = gate_inv[rows][:, 0:1]
        gnorm = yv * act * inv
        dn = d_normed[rows]
        prod = dn * gnorm
        acc[...] += prod
        dgn = dn * gain[...]
        mean = jnp.mean(dgn * gnorm, axis=1, keepdims=True)
        d_gated = inv * (dgn - gnorm * mean)
        d_y[rows] = d_gated * act
        d_gate[rows] = (d_gated * yv * (sig * (1.0 + g * (1.0 - sig)))).astype(BF16)

    gain_grad[...] = jnp.sum(acc[...], axis=0, keepdims=True)

    @pl.loop(0, 3)
    def _(j):
        cols = pl.ds(pl.multiple_of(j * 256, 256), 256)
        for lr in range(2):
            src = pl.ds(pl.multiple_of(j * 256 + lr * D, 256), 256)
            g = dot_tn(hidden[...], d_gate[:, src]).astype(BF16)
            for zx in range(16):
                grads[core, slot_of(0, z0, x0, zx), lr * 48 : lr * 48 + 48, cols] = g[
                    zx * 48 : zx * 48 + 48
                ]

    for t in range(4):
        g = dot_tn(normed[:, t * 384 : (t + 1) * 384], cot[...]).astype(BF16)
        for k in range(4):
            grads[1 - core, slot_of(1, z0, x0, t * 4 + k)] = g[k * 96 : (k + 1) * 96]

    @pl.loop(0, 3)
    def _(j):
        cols = pl.ds(pl.multiple_of(j * 256, 256), 256)
        right = pl.ds(pl.multiple_of(j * 256 + D, 256), 256)
        d_hid[:, cols] = dot_nt(d_gate[:, :D], weights[cols]) + dot_nt(
            d_gate[:, D:], weights[right]
        )


def kernel_c(
    pos, xs, bc, acum, bcum, dt_pre, d_y, y, conv_in, slope, conv_w, rate, d_skip, hidden,
    grads, d_proj, g_conv_w, g_conv_b, g_skip, g_dt, g_alog,
    d_conv, score_t, acum_t, d_score, rsum, csum,
):
    z0, x0, core = pos[0], pos[1], pos[2]
    above = iota((LEN, LEN), 0) <= iota((LEN, LEN), 1)
    upper = jnp.where(above, 1.0, 0.0)
    mask0, mask1 = head_masks()
    lane_head = iota((128, 128), 0) // 64
    head_col = iota((128, 128), 1)
    g_skip[...] = jnp.zeros_like(g_skip)
    g_dt[...] = jnp.zeros_like(g_dt)
    g_alog[...] = jnp.zeros_like(g_alog)
    d_proj[:, CONV_CH + 128 :] = jnp.zeros((ROWS, 128), BF16)

    for s in range(SEQS):
        rows = slice(s * LEN, (s + 1) * LEN)
        d_conv[s, LEN:] = jnp.zeros((8, CONV_CH), F32)
        acum_t[...] = acum[rows].T
        score_t[...] = jnp.where(above, dot_nt(bc[rows, :DS], bc[rows, DS:]), 0.0)
        d_score[...] = jnp.zeros_like(d_score)
        rsum[...] = jnp.zeros_like(rsum)
        csum[...] = jnp.zeros_like(csum)
        b = bcum[rows]

        @pl.loop(0, NH // 2)
        def _(p):
            lanes = pl.ds(pl.multiple_of(p * 128, 128), 128)
            x = xs[s * LEN : (s + 1) * LEN, lanes]
            dy = d_y[s * LEN : (s + 1) * LEN, lanes]
            ds = dy.astype(BF16)
            turned = pltpu.roll(b, lax.rem(128 - 2 * p, 128), 1)
            top = jnp.zeros((128, 128), F32)
            low = jnp.zeros((128, 128), F32)
            for i, mask in enumerate((mask0, mask1)):
                col = turned[:, i : i + 1]
                row = acum_t[pl.ds(2 * p + i, 1), :]
                dm = ds * mask
                xm = x * mask
                e0 = jnp.exp2(jnp.minimum(row - col[:128], 64.0))
                m0 = (e0 * score_t[:128, :]).astype(BF16)
                top = top + dot_nn(m0, dm)
                d_score[:128, :] += dot_nt(xm[:128], ds) * e0
                e1 = jnp.exp2(jnp.minimum(row[:, 128:] - col[128:], 64.0))
                m1 = (e1 * score_t[128:, 128:]).astype(BF16)
                low = low + dot_nn(m1, dm[128:])
                d_score[128:, 128:] += dot_nt(xm[128:], ds[128:]) * e1
            dxs = jnp.concatenate([top, low], axis=0)
            skip = d_skip[:, lanes]
            xf = x.astype(F32)
            own = ds.astype(F32) * (y[s * LEN : (s + 1) * LEN, lanes] - skip * xf)
            across = xf * dxs
            pick = jnp.where(lane_head + 2 * p == head_col, 1.0, 0.0)
            rsum[...] += dot_exact(own, pick)
            csum[...] += dot_exact(across, pick)
            g_skip[:, lanes] += jnp.sum(dy * xf, axis=0, keepdims=True)
            d_conv[s, 0:LEN, lanes] = (skip * dy + dxs) * slope[
                s * LEN : (s + 1) * LEN, lanes
            ]

        pre = dt_pre[rows]
        step = softplus(pre)
        sig = 1.0 / (1.0 + jnp.exp(-pre))
        ratio = jnp.where(pre < -20.0, 1.0, sig / jnp.maximum(step, 1e-30))
        d_cum = rsum[...] - csum[...]
        d_inc = dot_exact(upper, d_cum)
        g_alog[...] += jnp.sum(d_inc * step, axis=0, keepdims=True) * rate[...]
        d_pre = csum[...] * ratio + d_inc * rate[...] * sig
        g_dt[...] += jnp.sum(d_pre, axis=0, keepdims=True)
        d_proj[rows, CONV_CH : CONV_CH + 128] = d_pre.astype(BF16)
        dsc = jnp.where(above, d_score[...], 0.0).astype(BF16)
        d_b = dot_nn(dsc, bc[rows, DS:])
        d_c = dot_tn(dsc, bc[rows, :DS])
        d_conv[s, 0:LEN, DI : DI + DS] = d_b * slope[rows, DI : DI + DS]
        d_conv[s, 0:LEN, DI + DS :] = d_c * slope[rows, DI + DS :]

    @pl.loop(0, CONV_CH // 256)
    def _(j):
        cols = pl.ds(pl.multiple_of(j * 256, 256), 256)
        w = conv_w[:, cols]
        zero = jnp.zeros((8, 256), F32)
        sums = (zero,) * (CONV + 1)
        for s in range(SEQS):

            def chunk(i, sums):
                base = pl.multiple_of(i * 32, 32)
                later = d_conv[s, pl.ds(base, 40), cols]
                near = conv_in[s, pl.ds(base, 40), cols]
                here = later[0:32]
                back = w[CONV - 1 : CONV] * here
                for k in range(CONV - 1):
                    back = back + w[k : k + 1] * later[3 - k : 35 - k]
                d_proj[pl.ds(pl.multiple_of(s * LEN + base, 32), 32), cols] = back.astype(BF16)

                def fold(v):
                    return (v[0:8] + v[8:16]) + (v[16:24] + v[24:32])

                new = [sums[k] + fold(here * near[5 + k : 37 + k]) for k in range(CONV)]
                return tuple(new) + (sums[CONV] + fold(here),)

            sums = lax.fori_loop(0, LEN // 32, chunk, sums)
        for k in range(CONV):
            g_conv_w[k : k + 1, cols] = jnp.sum(sums[k], axis=0, keepdims=True)
        g_conv_b[:, cols] = jnp.sum(sums[CONV], axis=0, keepdims=True)

    @pl.loop(0, 4)
    def _(j):
        cols = pl.ds(pl.multiple_of(j * 256, 256), 256)
        for half in range(2):
            src = pl.ds(pl.multiple_of(j * 256 + half * HALF1, 256), 256)
            g = dot_tn(hidden[...], d_proj[:, src]).astype(BF16)
            side = jnp.where(core == half, 0, 1)
            for zx in range(16):
                grads[side, slot_of(half, z0, x0, zx), :, cols] = g[zx * 48 : zx * 48 + 48]


def kernel_d(d_proj, w1, d_hid, tokens, gain, cot, grad_tokens, gain_grad, d_full):
    @pl.loop(0, 3)
    def _(j):
        cols = pl.ds(pl.multiple_of(j * 256, 256), 256)
        d_full[:, cols] = d_hid[:, cols] + dot_nt(d_proj[...], w1[cols])

    def chunk(i, total):
        rows = pl.ds(pl.multiple_of(i * 32, 32), 32)
        t = tokens[rows].astype(F32)
        inv = lax.rsqrt(jnp.mean(t * t, axis=1, keepdims=True) + EPS)
        normal = t * inv
        dh = d_full[rows]
        prod = dh * normal
        dn = dh * gain[...]
        mean = jnp.mean(dn * normal, axis=1, keepdims=True)
        grad_tokens[rows] = cot[rows].astype(F32) + inv * (dn - normal * mean)
        return total + (prod[0:8] + prod[8:16]) + (prod[16:24] + prod[24:32])

    total = lax.fori_loop(0, ROWS // 32, chunk, jnp.zeros((8, D), F32))
    gain_grad[...] = jnp.sum(total, axis=0, keepdims=True)


VM = pl.BlockSpec(memory_space=pltpu.VMEM)
SM = pl.BlockSpec(memory_space=pltpu.SMEM)
HB = pl.BlockSpec(memory_space=pl.ANY)


def call(kernel, name, ins, outs, scratch, args, flops, nbytes):
    return pl.pallas_call(
        kernel,
        name=name,
        in_specs=ins,
        out_specs=[VM] * len(outs),
        out_shape=[jax.ShapeDtypeStruct(s, d) for s, d in outs],
        scratch_shapes=scratch,
        compiler_params=pltpu.CompilerParams(vmem_limit_bytes=LIMIT),
        cost_estimate=pl.CostEstimate(flops=flops, bytes_accessed=nbytes, transcendentals=0),
    )(*args)


def lanes24(v):
    return jnp.pad(v, (0, 128 - NH)).reshape(1, 128)


def per_device(
    tokens,
    in_weight,
    out_weight,
    norm_gain,
    conv_weight,
    conv_bias,
    dt_bias,
    a_log,
    d_skip,
    gated_gain,
    cotangent,
):
    me = lax.axis_index("fsdp")
    core = lax.rem(me, 2)
    pos = jnp.stack([me // 32, lax.rem(me // 8, 4), core]).astype(jnp.int32)

    win = in_weight.reshape(6, NCOL)
    conv_cols = jnp.pad(win[:, DI:], ((0, 0), (0, WIDE1 - (NCOL - DI))))
    halves = jnp.stack(
        [
            jnp.concatenate([conv_cols[:, :HALF1], win[:, :DI]], axis=1),
            jnp.concatenate([conv_cols[:, HALF1:], out_weight.reshape(6, DI)], axis=1),
        ]
    )
    sent = jnp.broadcast_to(halves[None], (4, 2, 6, HALF1 + DI)).reshape(8, 6, HALF1 + DI)
    eight = lax.all_to_all(sent, "fsdp", 0, 0, axis_index_groups=EIGHTS)
    first = eight[:, :, :HALF1].reshape(48, HALF1)
    second = eight[:, :, HALF1:]
    as_gate = jnp.concatenate(
        [second[:, :, :D].reshape(48, D), second[:, :, D:].reshape(48, D)], axis=0
    )
    second = jnp.where(core == 0, as_gate, second.reshape(96, D))

    own1 = ring_gather(jnp.concatenate(ring_gather(first, False), axis=0), True)
    other1 = [swap_core(v) for v in own1]
    own2 = ring_gather(jnp.concatenate(ring_gather(second, False), axis=0), True)
    other2 = [swap_core(v) for v in own2]

    gain = norm_gain.reshape(1, D)
    rate = lanes24(-jnp.exp(a_log))
    skip = jnp.repeat(d_skip, HEAD).reshape(1, DI)
    tap_bias = conv_bias.reshape(1, CONV_CH)

    hidden, w1, conv_in, slope, xs, bc, dt_pre, acum, bcum, y = call(
        kernel_a,
        "forward_ssd",
        [SM] + [VM] * 7 + [HB] * 8,
        [
            ((ROWS, D), BF16),
            ((D, WIDE1), BF16),
            ((SEQS, PADLEN, CONV_CH), F32),
            ((ROWS, CONV_CH), F32),
            ((ROWS, DI), BF16),
            ((ROWS, 2 * DS), BF16),
            ((ROWS, 128), F32),
            ((ROWS, 128), F32),
            ((ROWS, 128), F32),
            ((ROWS, DI), F32),
        ],
        [
            pltpu.VMEM((LEN, LEN), F32),
            pltpu.VMEM((128, LEN), F32),
            pltpu.SemaphoreType.DMA((2, 4, 4)),
        ],
        [pos, tokens, gain, conv_weight, tap_bias, lanes24(dt_bias), rate, skip] + own1 + other1,
        8_000_000_000,
        20_000_000,
    )

    out, d_y, grads2, d_hid, g_gated = call(
        kernel_b,
        "gate_output",
        [SM] + [VM] * 5 + [HB] * 8,
        [
            ((ROWS, D), BF16),
            ((ROWS, DI), F32),
            ((2, 16, 96, D), BF16),
            ((ROWS, D), F32),
            ((1, DI), F32),
        ],
        [
            pltpu.VMEM((2 * DI, D), BF16),
            pltpu.VMEM((ROWS, DI), F32),
            pltpu.VMEM((ROWS, DI), F32),
            pltpu.VMEM((ROWS, DI), BF16),
            pltpu.VMEM((ROWS, DI), BF16),
            pltpu.VMEM((ROWS, 128), F32),
            pltpu.VMEM((16, DI), F32),
            pltpu.SemaphoreType.DMA((2, 4, 4, 2)),
        ],
        [pos, hidden, y, tokens, cotangent, gated_gain.reshape(1, DI)] + own2 + other2,
        9_000_000_000,
        20_000_000,
    )

    sum2 = grads2[0].astype(F32) + swap_core(grads2[1]).astype(F32)
    sum2 = sum2.reshape(4, 4, 96, D)
    sum2 = ring_reduce([sum2[r] for r in range(4)], True)
    sum2 = ring_reduce([sum2[r] for r in range(4)], False)
    as_gate = sum2.reshape(2, 8, 6, D).swapaxes(0, 1).reshape(8, 12, D)
    sum2 = jnp.where(core == 0, as_gate, sum2.reshape(8, 12, D)).astype(BF16)
    back2 = lax.all_to_all(sum2, "fsdp", 0, 0, axis_index_groups=EIGHTS)
    back2 = jnp.sum(back2.reshape(4, 2, 12, D).astype(F32), axis=0)
    grad_gate = back2[0].reshape(2, 6, D).swapaxes(0, 1).reshape(6, DI)
    grad_out = back2[1].reshape(-1)

    grads1, d_proj, g_conv_w, g_conv_b, g_skip, g_dt, g_alog = call(
        kernel_c,
        "backward_ssd",
        [SM] + [VM] * 13,
        [
            ((2, 16, 48, HALF1), BF16),
            ((ROWS, WIDE1), BF16),
            ((CONV, CONV_CH), F32),
            ((1, CONV_CH), F32),
            ((1, DI), F32),
            ((1, 128), F32),
            ((1, 128), F32),
        ],
        [
            pltpu.VMEM((SEQS, PADLEN, CONV_CH), F32),
            pltpu.VMEM((LEN, LEN), F32),
            pltpu.VMEM((128, LEN), F32),
            pltpu.VMEM((LEN, LEN), F32),
            pltpu.VMEM((LEN, 128), F32),
            pltpu.VMEM((LEN, 128), F32),
        ],
        [pos, xs, bc, acum, bcum, dt_pre, d_y, y, conv_in, slope, conv_weight, rate, skip, hidden],
        8_000_000_000,
        30_000_000,
    )

    grad_tokens, g_norm = call(
        kernel_d,
        "grad_tokens",
        [VM] * 6,
        [((ROWS, D), F32), ((1, D), F32)],
        [pltpu.VMEM((ROWS, D), F32)],
        [d_proj, w1, d_hid, tokens, gain, cotangent],
        2_000_000_000,
        10_000_000,
    )

    small = jnp.concatenate(
        [
            g_norm.reshape(-1),
            g_conv_w.reshape(-1),
            g_conv_b.reshape(-1),
            g_dt[0, :NH],
            g_alog[0, :NH],
            jnp.sum(g_skip.reshape(NH, HEAD), axis=1),
            g_gated.reshape(-1),
        ]
    )
    count = small.shape[0]
    small = jnp.pad(small, (0, 12 * HALF1 - count)).reshape(12, HALF1)

    def split(v):
        hi = lax.reduce_precision(v, 8, 7)
        return jnp.concatenate([hi.astype(BF16), (v - hi).astype(BF16)], axis=0)

    def joined(v):
        return v[..., :12, :].astype(F32) + v[..., 12:, :].astype(F32)

    def reduce_with_small(parts, extra, last):
        packed = jnp.pad(split(extra), ((0, 8), (0, 0)))
        got, more = [parts[0].astype(F32)], [joined(packed[:24])]
        for r in (1, 2, 3):
            there = lax.ppermute(
                jnp.concatenate([parts[r].astype(BF16), packed], axis=0),
                "fsdp",
                ring_pairs(r, last),
            )
            got.append(there[:-32].astype(F32))
            more.append(joined(there[-32:-8]))
        return (got[0] + got[2]) + (got[1] + got[3]), (more[0] + more[2]) + (more[1] + more[3])

    sum1 = grads1[0].astype(F32) + swap_core(grads1[1]).astype(F32)
    sum1 = sum1.reshape(4, 192, HALF1)
    sum1, small = reduce_with_small([sum1[r] for r in range(4)], small, True)
    sum1 = sum1.reshape(4, 48, HALF1)
    sum1, small = reduce_with_small([sum1[r] for r in range(4)], small, False)
    packed = jnp.concatenate(
        [
            jnp.broadcast_to(split(small)[None], (8, 24, HALF1)),
            sum1.reshape(8, 6, HALF1).astype(BF16),
            jnp.zeros((8, 2, HALF1), BF16),
        ],
        axis=1,
    )
    back1 = lax.all_to_all(packed, "fsdp", 0, 0, axis_index_groups=EIGHTS)
    small = jnp.sum(joined(back1[:, :24]), axis=0).reshape(-1)
    back1 = jnp.sum(back1[:, 24:30].reshape(4, 2, 6, HALF1).astype(F32), axis=0)
    grad_in = jnp.concatenate(
        [grad_gate, back1[0], back1[1][:, : NCOL - DI - HALF1]], axis=1
    ).reshape(-1)

    pieces = []
    start = 0
    for size in (D, CONV * CONV_CH, CONV_CH, NH, NH, NH, DI):
        pieces.append(small[start : start + size])
        start += size
    pieces[1] = pieces[1].reshape(CONV, CONV_CH)
    return (out, grad_tokens, grad_in, grad_out) + tuple(pieces)


def solution(mesh):
    rows = P("fsdp", None)
    flat = P("fsdp")
    same = P()
    return jax.shard_map(
        per_device,
        mesh=mesh,
        in_specs=(rows, flat, flat) + (same,) * 7 + (rows,),
        out_specs=(rows, rows, flat, flat) + (same,) * 7,
        check_vma=False,
    )
```

time: 526 us -> 259 us (0.49); the launches traced: 516 us -> 258 us
  waiting for transfers between devices: 252 us -> 49.1 us
  Pallas kernels: 0 us -> 101 us
  starting transfers between devices: 0.12 us -> 70.7 us
  blocking collectives: 65.7 us -> 0 us
  matrix products: 58.6 us -> 0 us
  local copies, waits for them, and re-layouts: 77 us -> 22.2 us
  other arithmetic: 48.4 us -> 12.7 us
  between operations: 14.7 us -> 1.41 us
    unnamed x5 -> x0, waiting for transfers between devices: 252 us -> none
    pallas_call x0 -> x4, Pallas kernels: none -> 101 us  [call(): pl.pallas_call(kernel, name=name, in_specs=ins, out_specs=[VM] * len(outs...]
    psum x1 -> x0, blocking collectives: 65.7 us -> none  [per_device(): lax.psum((grad_norm_gain, grad_conv_weight, grad_conv_bias, grad_dt_bias,...]
    dot_general x12 -> x0, matrix products: 58.6 us -> none  [the longest x1 10.5 us: per_device(): jnp.einsum('sthp,suhp->shtu', d_ssd, heads_x, preferred_element_type=jnp....]
    ppermute x0 -> x34, starting transfers between devices: none -> 51.8 us  [the longest x10 24 us: swap_core(): return lax.ppermute(value, 'fsdp', CORE_PAIRS)]
    reshape x9 -> x19, local copies, waits for them, and re-layouts: 48.7 us -> 6.91 us  [the longest x2 1.11 us: lanes24(): return jnp.pad(v, (0, 128 - NH)).reshape(1, 128)]
    ppermute x0 -> x34, waiting for transfers between devices: none -> 37.3 us  [the longest x6 13.7 us: ring_reduce(): lax.ppermute(parts[r].astype(BF16), 'fsdp', ring_pairs(r, last)).astype(F32)]
    reduce_sum x6 -> x4, other arithmetic: 23.4 us -> 0.3 us  [the longest x1 0.12 us: per_device(): small = jnp.sum(joined(back1[:, :24]), axis=0).reshape(-1)]
  transfers between devices with their start and end apart: 3 -> 37, of which waited for: 2 -> 16; matrix products, arithmetic and copies ran while one was open for 16% -> 8% of each run, Pallas kernels for 0% -> 15%
where the time goes in v1:
time: 259 us; the launch traced here: 258 us
  Pallas kernels  101 us (39%)
  starting transfers between devices  70.7 us (27%)
  waiting for transfers between devices  49.1 us (19%)
  local copies, waits for them, and re-layouts  22.2 us (9%)
  other arithmetic  12.7 us (5%)
    pallas_call x4, Pallas kernels, call(): pl.pallas_call(kernel, name=name, in_specs=ins, out_specs=[VM] * len(outs...  101 us
    ppermute x10, starting transfers between devices, swap_core(): return lax.ppermute(value, 'fsdp', CORE_PAIRS)  24 us
    ppermute x12, starting transfers between devices, ring_gather(): lax.ppermute(value, 'fsdp', ring_pairs(shift, last))  15.9 us
    ppermute x6, waiting for transfers between devices, ring_reduce(): lax.ppermute(parts[r].astype(BF16), 'fsdp', ring_pairs(r, last)).astype(F32)  13.7 us
    ppermute x6, waiting for transfers between devices, reduce_with_small(): lax.ppermute(jnp.concatenate([parts[r].astype(BF16), packed], axis=0), 'f...  12.5 us
    ppermute x12, waiting for transfers between devices, ring_gather(): lax.ppermute(value, 'fsdp', ring_pairs(shift, last))  11.1 us
    ppermute x6, starting transfers between devices, reduce_with_small(): lax.ppermute(jnp.concatenate([parts[r].astype(BF16), packed], axis=0), 'f...  7.11 us
    all_to_all x1, waiting for transfers between devices, per_device(): eight = lax.all_to_all(sent, 'fsdp', 0, 0, axis_index_groups=EIGHTS)  7.06 us
  transfers between devices with their start and end apart: 37, of which 16 were waited for; matrix products, arithmetic and copies ran while one was open for 8% of the time, Pallas kernels for 15%

profile of v1, /device:TPU:1, one launch (start us, length us, event | category | flops | bytes accessed | tf_op | source)
XLA Modules:
  0.0 257.6 jit_solution(6225478268357624699)
XLA Ops:
  3.2 6.0 %all-to-all-start = ((bf16[8,6,2560]{2,1,0:T(8,128)(2,1)}), bf16[8,6,2560]{2,1,0:T(8,128)(2,1)S(1)}, u32[]{:S(2)}, u32[]{:S(2)}) async-start(bf16[8,6,2560]{2,1,0:T(8,128)(2,1)} %bitcast.7), calls=%async_computation | async-start | bytes 655360 | tf_op jit(solution)/shard_map/all_to_all | solution.py:520
  9.2 7.1 %all-to-all-done = bf16[8,6,2560]{2,1,0:T(8,128)(2,1)S(1)} async-done(((bf16[8,6,2560]{2,1,0:T(8,128)(2,1)}), bf16[8,6,2560]{2,1,0:T(8,128)(2,1)S(1)}, u32[]{:S(2)}, u32[]{:S(2)}) %all-to-all-start) | async-done | bytes 245792 | tf_op jit(solution)/shard_map/all_to_all | solution.py:520
  18.0 3.3 %collective-permute-start.1 = (bf16[48,1024]{1,0:T(8,128)(2,1)S(1)}, bf16[48,1024]{1,0:T(8,128)(2,1)S(1)}, u32[]{:S(2)}, u32[]{:S(2)}) collective-permute-start(bf16[48,1024]{1,0:T(8,128)(2,1)S(1)} %reshape.151), channel_id=1, source_target_pairs={{0,16},{1,65},{2,18},{3,67},{4,20},{5,69},{6,22},{7,71},{8,24},{9,... | collective-permute-start | bytes 294920 | tf_op jit(solution)/shard_map/ppermute | solution.py:57
  22.4 2.5 collective-permute-start.11
  36.1 6.1 %collective-permute-start.6 = (bf16[192,1024]{1,0:T(8,128)(2,1)S(1)}, bf16[192,1024]{1,0:T(8,128)(2,1)S(1)}, u32[]{:S(2)}, u32[]{:S(2)}) collective-permute-start(bf16[192,1024]{1,0:T(8,128)(2,1)S(1)} %constant_dynamic-update-slice_fusion.b0), channel_id=1, source_target_pairs={{0,1},{1,0},{2,3},{3,2},{4,5},{5,4},{6,7},{7,6},{8,9},{9,8},{10,11... | collective-permute-start | bytes 1179656 | tf_op jit(solution)/shard_map/ppermute | solution.py:70
  42.2 2.5 collective-permute-done.3.b1
  46.4 3.4 %collective-permute-done.4.b2 = bf16[192,1024]{1,0:T(8,128)(2,1)} collective-permute-done((bf16[192,1024]{1,0:T(8,128)(2,1)S(1)}, bf16[192,1024]{1,0:T(8,128)(2,1)}, u32[]{:S(2)}, u32[]{:S(2)}) %collective-permute-start.4) | collective-permute-done | bytes 393248 | tf_op jit(solution)/shard_map/ppermute | solution.py:57
  52.8 6.1 %collective-permute-start.7 = (bf16[192,1024]{1,0:T(8,128)(2,1)}, bf16[192,1024]{1,0:T(8,128)(2,1)S(1)}, u32[]{:S(2)}, u32[]{:S(2)}) collective-permute-start(bf16[192,1024]{1,0:T(8,128)(2,1)} %collective-permute-done.3.b1), channel_id=1, source_target_pairs={{0,1},{1,0},{2,3},{3,2},{4,5},{5,4},{6,7},{7,6},{8,9},{9,8},{10,11... | collective-permute-start | bytes 1179656 | tf_op jit(solution)/shard_map/ppermute | solution.py:70
  60.7 2.5 collective-permute-start.16
  63.2 4.1 %collective-permute-start.17 = (bf16[384,768]{1,0:T(8,128)(2,1)S(1)}, bf16[384,768]{1,0:T(8,128)(2,1)S(1)}, u32[]{:S(2)}, u32[]{:S(2)}) collective-permute-start(bf16[384,768]{1,0:T(8,128)(2,1)S(1)} %collective-permute-done.13.b1), channel_id=1, source_target_pairs={{0,1},{1,0},{2,3},{3,2},{4,5},{5,4},{6,7},{7,6},{8,9},{9,8},{10,11... | collective-permute-start | bytes 1769480 | tf_op jit(solution)/shard_map/ppermute | solution.py:70
  68.2 27.6 %forward_ssd.1 = (bf16[512,768]{1,0:T(8,128)(2,1)}, bf16[768,2048]{1,0:T(8,128)(2,1)}, f32[2,264,1792]{2,1,0:T(8,128)}, f32[512,1792]{1,0:T(8,128)}, bf16[512,15...) custom-call(s32[3]{0:T(128)} %pad_add_fusion.pos, ...), custom_call_target="tpu_custom_call" | custom-call | flops 8000000000 | bytes 20000000 | tf_op jit(solution)/shard_map/forward_ssd/pallas_call | solution.py:478
  97.4 30.2 %gate_output.1 = (bf16[512,768]{1,0:T(8,128)(2,1)}, f32[512,1536]{1,0:T(8,128)}, bf16[2,16,96,768]{3,2,1,0:T(8,128)(2,1)}, f32[512,768]{1,0:T(8,128)}, f32[1,1536]{1,0:T(1,128)}) custom-call(s32[3]{0:T(128)} %pad_add_fusion.pos, bf16[512,768]{1,0:T(8,128)(2,1)} %get-tuple-element.35.hidden, f32[512,1536]{1,0:T(8,128)} %get-tuple-element.36.y, ...), custom_call_target="tpu_custom_call" | custom-call | flops 8999999488 | bytes 20000000 | tf_op jit(solution)/shard_map/gate_output/pallas_call | solution.py:478
  127.6 33.5 %backward_ssd.1 = (bf16[2,16,48,1024]{3,2,1,0:T(8,128)(2,1)}, bf16[512,2048]{1,0:T(8,128)(2,1)}, f32[4,1792]{1,0:T(4,128)}, f32[1,1792]{1,0:T(1,128)}, f32[1,153...) custom-call(s32[3]{0:T(128)} %pad_add_fusion.pos, bf16[512,1536]{1,0:T(8,128)(2,1)} %get-tuple-element.38.xs, ...), custom_call_target="tpu_custom_call" | custom-call | flops 8000000000 | bytes 30000000 | tf_op jit(solution)/shard_map/backward_ssd/pallas_call | solution.py:478
  161.1 2.8 %slice_bitcast_fusion.1 = bf16[16,48,1024]{2,1,0:T(8,128)(2,1)} fusion(bf16[2,16,48,1024]{3,2,1,0:T(8,128)(2,1)} %get-tuple-element.58), kind=kLoop, calls=%fused_computation.3 | loop fusion | bytes 3145728 | tf_op jit(solution)/shard_map/squeeze | solution.py:672
  164.3 10.1 %grad_tokens.1 = (f32[512,768]{1,0:T(8,128)}, f32[1,768]{1,0:T(1,128)}) custom-call(bf16[512,2048]{1,0:T(8,128)(2,1)} %get-tuple-element.46.d_proj, bf16[768,2048]{1,0:T(8,128)(2,1)} %get-tuple-element.47.w1, f32[512,768]{1,0:T(8,128)} %get-tuple-element.48.d_hid, bf16[512,768]{1,0:T(8,128)(2,1)} %tokens.5, f32[1,768]{1,0:T(1,128)} %reshape.144.gain, ...), custom_call_target="tpu_custom_call" | custom-call | flops 2000000000 | bytes 10000000 | tf_op jit(solution)/shard_map/grad_tokens/pallas_call | solution.py:478
  180.6 3.8 %collective-permute-start.20 = (bf16[16,96,768]{2,1,0:T(8,128)(2,1)S(1)}, bf16[16,96,768]{2,1,0:T(8,128)(2,1)}, u32[]{:S(2)}, u32[]{:S(2)}) collective-permute-start(bf16[16,96,768]{2,1,0:T(8,128)(2,1)S(1)} %slice_bitcast_fusion), channel_id=1, source_target_pairs={{0,1},{1,0},{2,3},{3,2},{4,5},{5,4},{6,7},{7,6},{8,9},{9,8},{10,11... | collective-permute-start | bytes 7077896 | tf_op jit(solution)/shard_map/ppermute | solution.py:70
  185.8 6.2 %collective-permute-done.29 = bf16[224,1024]{1,0:T(8,128)(2,1)S(1)} collective-permute-done((bf16[224,1024]{1,0:T(8,128)(2,1)S(1)}, bf16[224,1024]{1,0:T(8,128)(2,1)S(1)}, u32[]{:S(2)}, u32[]{:S(2)}) %collective-permute-start.29) | collective-permute-done | bytes 458784 | tf_op jit(solution)/shard_map/ppermute | solution.py:663
  194.9 2.4 collective-permute-start.31
  197.4 4.9 %collective-permute-done.32 = bf16[80,1024]{1,0:T(8,128)(2,1)S(1)} collective-permute-done((bf16[80,1024]{1,0:T(8,128)(2,1)S(1)}, bf16[80,1024]{1,0:T(8,128)(2,1)S(1)}, u32[]{:S(2)}, u32[]{:S(2)}) %collective-permute-start.32) | collective-permute-done | bytes 163872 | tf_op jit(solution)/shard_map/ppermute | solution.py:663
  203.6 6.0 %all-to-all-start.2 = ((bf16[8,32,1024]{2,1,0:T(8,128)(2,1)}), bf16[8,32,1024]{2,1,0:T(8,128)(2,1)S(1)}, u32[]{:S(2)}, u32[]{:S(2)}) async-start(bf16[8,32,1024]{2,1,0:T(8,128)(2,1)} %maximum_maximum_fusion), calls=%async_computation.2 | async-start | bytes 1048576 | tf_op jit(solution)/shard_map/all_to_all | solution.py:685
  209.6 5.3 %convert_add_fusion = (f32[16,96,768]{2,1,0:T(8,128)}, bf16[16,96,768]{2,1,0:T(8,128)(2,1)S(1)}) fusion(bf16[16,96,768]{2,1,0:T(8,128)(2,1)} %collective-permute-done.20, bf16[2,16,96,768]{3,2,1,0:T(8,128)(2,1)} %get-tuple-element.50), kind=kLoop, calls=%fused_computation | loop fusion | flops 4718592 | bytes 11796480 | tf_op jit(solution)/shard_map/add | solution.py:590
  225.0 8.4 %collective-permute-done.22 = bf16[4,96,768]{2,1,0:T(8,128)(2,1)S(1)} collective-permute-done((bf16[4,96,768]{2,1,0:T(8,128)(2,1)S(1)}, bf16[4,96,768]{2,1,0:T(8,128)(2,1)S(1)}, u32[]{:S(2)}, u32[]{:S(2)}) %collective-permute-start.22) | collective-permute-done | bytes 589856 | tf_op jit(solution)/shard_map/ppermute | solution.py:63
  243.3 6.9 %all-to-all-start.1 = ((bf16[8,12,768]{2,1,0:T(8,128)(2,1)}), bf16[8,12,768]{2,1,0:T(8,128)(2,1)S(1)}, u32[]{:S(2)}, u32[]{:S(2)}) async-start(bf16[8,12,768]{2,1,0:T(8,128)(2,1)} %copy.37), calls=%async_computation.1 | async-start | bytes 393216 | tf_op jit(solution)/shard_map/all_to_all | solution.py:596
  251.6 4.5 %all-to-all-done.1 = bf16[8,12,768]{2,1,0:T(8,128)(2,1)S(1)} async-done(((bf16[8,12,768]{2,1,0:T(8,128)(2,1)}), bf16[8,12,768]{2,1,0:T(8,128)(2,1)S(1)}, u32[]{:S(2)}, u32[]{:S(2)}) %all-to-all-start.1) | async-done | bytes 147488 | tf_op jit(solution)/shard_map/all_to_all | solution.py:596
  (203 shorter events, 60.1 us)
Async XLA Ops:
  3.2 13.1 %all-to-all-start = ((bf16[8,6,2560]{2,1,0:T(8,128)(2,1)}), bf16[8,6,2560]{2,1,0:T(8,128)(2,1)S(1)}, u32[]{:S(2)}, u32[]{:S(2)}) async-start(bf16[8,6,2560]{2,1,0:T(8,128)(2,1)} %bitcast.7), calls=%async_computation | async-start | bytes 655360 | tf_op jit(solution)/shard_map/all_to_all | solution.py:520
  21.3 10.3 %collective-permute-start.2 = (bf16[48,1024]{1,0:T(8,128)(2,1)S(1)}, bf16[48,1024]{1,0:T(8,128)(2,1)S(1)}, u32[]{:S(2)}, u32[]{:S(2)}) collective-permute-start(bf16[48,1024]{1,0:T(8,128)(2,1)S(1)} %reshape.151), channel_id=1, source_target_pairs={{0,24},{1,97},{2,26},{3,99},{4,28},{5,101},{6,30},{7,103},{8,0},{9... | collective-permute-start | bytes 294920 | tf_op jit(solution)/shard_map/ppermute | solution.py:57
  30.2 28.8 %collective-permute-start.13 = (bf16[384,768]{1,0:T(8,128)(2,1)S(1)}, bf16[384,768]{1,0:T(8,128)(2,1)S(1)}, u32[]{:S(2)}, u32[]{:S(2)}) collective-permute-start(bf16[384,768]{1,0:T(8,128)(2,1)S(1)} %pad_maximum_fusion.3.b0), channel_id=1, source_target_pairs={{0,32},{1,9},{2,34},{3,11},{4,36},{5,13},{6,38},{7,15},{8,40},{9,1... | collective-permute-start | bytes 1769480 | tf_op jit(solution)/shard_map/ppermute | solution.py:57
  31.6 13.1 %collective-permute-start.3 = (bf16[192,1024]{1,0:T(8,128)(2,1)S(1)}, bf16[192,1024]{1,0:T(8,128)(2,1)}, u32[]{:S(2)}, u32[]{:S(2)}) collective-permute-start(bf16[192,1024]{1,0:T(8,128)(2,1)S(1)} %constant_dynamic-update-slice_fusion.b0), channel_id=1, source_target_pairs={{0,32},{1,9},{2,34},{3,11},{4,36},{5,13},{6,38},{7,15},{8,40},{9,1... | collective-permute-start | bytes 1179656 | tf_op jit(solution)/shard_map/ppermute | solution.py:57
  32.8 16.9 %collective-permute-start.4 = (bf16[192,1024]{1,0:T(8,128)(2,1)S(1)}, bf16[192,1024]{1,0:T(8,128)(2,1)}, u32[]{:S(2)}, u32[]{:S(2)}) collective-permute-start(bf16[192,1024]{1,0:T(8,128)(2,1)S(1)} %constant_dynamic-update-slice_fusion.b0), channel_id=1, source_target_pairs={{0,64},{1,17},{2,66},{3,19},{4,68},{5,21},{6,70},{7,23},{8,72},{9,... | collective-permute-start | bytes 1179656 | tf_op jit(solution)/shard_map/ppermute | solution.py:57
  34.3 18.6 %collective-permute-start.5 = (bf16[192,1024]{1,0:T(8,128)(2,1)S(1)}, bf16[192,1024]{1,0:T(8,128)(2,1)}, u32[]{:S(2)}, u32[]{:S(2)}) collective-permute-start(bf16[192,1024]{1,0:T(8,128)(2,1)S(1)} %constant_dynamic-update-slice_fusion.b0), channel_id=1, source_target_pairs={{0,96},{1,25},{2,98},{3,27},{4,100},{5,29},{6,102},{7,31},{8,104},... | collective-permute-start | bytes 1179656 | tf_op jit(solution)/shard_map/ppermute | solution.py:57
  36.1 22.8 %collective-permute-start.6 = (bf16[192,1024]{1,0:T(8,128)(2,1)S(1)}, bf16[192,1024]{1,0:T(8,128)(2,1)S(1)}, u32[]{:S(2)}, u32[]{:S(2)}) collective-permute-start(bf16[192,1024]{1,0:T(8,128)(2,1)S(1)} %constant_dynamic-update-slice_fusion.b0), channel_id=1, source_target_pairs={{0,1},{1,0},{2,3},{3,2},{4,5},{5,4},{6,7},{7,6},{8,9},{9,8},{10,11... | collective-permute-start | bytes 1179656 | tf_op jit(solution)/shard_map/ppermute | solution.py:70
  44.8 15.9 %collective-permute-start.14 = (bf16[384,768]{1,0:T(8,128)(2,1)S(1)}, bf16[384,768]{1,0:T(8,128)(2,1)S(1)}, u32[]{:S(2)}, u32[]{:S(2)}) collective-permute-start(bf16[384,768]{1,0:T(8,128)(2,1)S(1)} %pad_maximum_fusion.3.b0), channel_id=1, source_target_pairs={{0,64},{1,17},{2,66},{3,19},{4,68},{5,21},{6,70},{7,23},{8,72},{9,... | collective-permute-start | bytes 1769480 | tf_op jit(solution)/shard_map/ppermute | solution.py:57
  49.8 13.4 %collective-permute-start.15 = (bf16[384,768]{1,0:T(8,128)(2,1)S(1)}, bf16[384,768]{1,0:T(8,128)(2,1)S(1)}, u32[]{:S(2)}, u32[]{:S(2)}) collective-permute-start(bf16[384,768]{1,0:T(8,128)(2,1)S(1)} %pad_maximum_fusion.3.b0), channel_id=1, source_target_pairs={{0,96},{1,25},{2,98},{3,27},{4,100},{5,29},{6,102},{7,31},{8,104},... | collective-permute-start | bytes 1769480 | tf_op jit(solution)/shard_map/ppermute | solution.py:57
  52.8 14.5 %collective-permute-start.7 = (bf16[192,1024]{1,0:T(8,128)(2,1)}, bf16[192,1024]{1,0:T(8,128)(2,1)S(1)}, u32[]{:S(2)}, u32[]{:S(2)}) collective-permute-start(bf16[192,1024]{1,0:T(8,128)(2,1)} %collective-permute-done.3.b1), channel_id=1, source_target_pairs={{0,1},{1,0},{2,3},{3,2},{4,5},{5,4},{6,7},{7,6},{8,9},{9,8},{10,11... | collective-permute-start | bytes 1179656 | tf_op jit(solution)/shard_map/ppermute | solution.py:70
  59.0 8.8 %collective-permute-start.9 = (bf16[192,1024]{1,0:T(8,128)(2,1)}, bf16[192,1024]{1,0:T(8,128)(2,1)}, u32[]{:S(2)}, u32[]{:S(2)}) collective-permute-start(bf16[192,1024]{1,0:T(8,128)(2,1)} %collective-permute-done.5.b3), channel_id=1, source_target_pairs={{0,1},{1,0},{2,3},{3,2},{4,5},{5,4},{6,7},{7,6},{8,9},{9,8},{10,11... | collective-permute-start | bytes 1179656 | tf_op jit(solution)/shard_map/ppermute | solution.py:70
  60.7 35.2 %collective-permute-start.16 = (bf16[384,768]{1,0:T(8,128)(2,1)S(1)}, bf16[384,768]{1,0:T(8,128)(2,1)S(1)}, u32[]{:S(2)}, u32[]{:S(2)}) collective-permute-start(bf16[384,768]{1,0:T(8,128)(2,1)S(1)} %pad_maximum_fusion.3.b0), channel_id=1, source_target_pairs={{0,1},{1,0},{2,3},{3,2},{4,5},{5,4},{6,7},{7,6},{8,9},{9,8},{10,11... | collective-permute-start | bytes 1769480 | tf_op jit(solution)/shard_map/ppermute | solution.py:70
  63.2 32.7 %collective-permute-start.17 = (bf16[384,768]{1,0:T(8,128)(2,1)S(1)}, bf16[384,768]{1,0:T(8,128)(2,1)S(1)}, u32[]{:S(2)}, u32[]{:S(2)}) collective-permute-start(bf16[384,768]{1,0:T(8,128)(2,1)S(1)} %collective-permute-done.13.b1), channel_id=1, source_target_pairs={{0,1},{1,0},{2,3},{3,2},{4,5},{5,4},{6,7},{7,6},{8,9},{9,8},{10,11... | collective-permute-start | bytes 1769480 | tf_op jit(solution)/shard_map/ppermute | solution.py:70
  67.3 28.6 %collective-permute-start.18 = (bf16[384,768]{1,0:T(8,128)(2,1)S(1)}, bf16[384,768]{1,0:T(8,128)(2,1)S(1)}, u32[]{:S(2)}, u32[]{:S(2)}) collective-permute-start(bf16[384,768]{1,0:T(8,128)(2,1)S(1)} %collective-permute-done.14.b2), channel_id=1, source_target_pairs={{0,1},{1,0},{2,3},{3,2},{4,5},{5,4},{6,7},{7,6},{8,9},{9,8},{10,11... | collective-permute-start | bytes 1769480 | tf_op jit(solution)/shard_map/ppermute | solution.py:70
  67.4 28.5 %collective-permute-start.19 = (bf16[384,768]{1,0:T(8,128)(2,1)S(1)}, bf16[384,768]{1,0:T(8,128)(2,1)S(1)}, u32[]{:S(2)}, u32[]{:S(2)}) collective-permute-start(bf16[384,768]{1,0:T(8,128)(2,1)S(1)} %collective-permute-done.15.b3), channel_id=1, source_target_pairs={{0,1},{1,0},{2,3},{3,2},{4,5},{5,4},{6,7},{7,6},{8,9},{9,8},{10,11... | collective-permute-start | bytes 1769480 | tf_op jit(solution)/shard_map/ppermute | solution.py:70
  163.8 11.7 %collective-permute-start.27 = (bf16[16,48,1024]{2,1,0:T(8,128)(2,1)}, bf16[16,48,1024]{2,1,0:T(8,128)(2,1)}, u32[]{:S(2)}, u32[]{:S(2)}) collective-permute-start(bf16[16,48,1024]{2,1,0:T(8,128)(2,1)} %slice_bitcast_fusion.1), channel_id=1, source_target_pairs={{0,1},{1,0},{2,3},{3,2},{4,5},{5,4},{6,7},{7,6},{8,9},{9,8},{10,11... | collective-permute-start | bytes 4718600 | tf_op jit(solution)/shard_map/ppermute | solution.py:70
  178.2 13.8 %collective-permute-start.29 = (bf16[224,1024]{1,0:T(8,128)(2,1)S(1)}, bf16[224,1024]{1,0:T(8,128)(2,1)S(1)}, u32[]{:S(2)}, u32[]{:S(2)}) collective-permute-start(bf16[224,1024]{1,0:T(8,128)(2,1)S(1)} %get-tuple-element.93), channel_id=1, source_target_pairs={{0,32},{1,9},{2,34},{3,11},{4,36},{5,13},{6,38},{7,15},{8,40},{9,1... | collective-permute-start | bytes 1376264 | tf_op jit(solution)/shard_map/ppermute | solution.py:663
  179.7 12.4 %collective-permute-start.28 = (bf16[224,1024]{1,0:T(8,128)(2,1)S(1)}, bf16[224,1024]{1,0:T(8,128)(2,1)S(1)}, u32[]{:S(2)}, u32[]{:S(2)}) collective-permute-start(bf16[224,1024]{1,0:T(8,128)(2,1)S(1)} %get-tuple-element.92), channel_id=1, source_target_pairs={{0,64},{1,17},{2,66},{3,19},{4,68},{5,21},{6,70},{7,23},{8,72},{9,... | collective-permute-start | bytes 1376264 | tf_op jit(solution)/shard_map/ppermute | solution.py:663
  180.6 29.0 %collective-permute-start.20 = (bf16[16,96,768]{2,1,0:T(8,128)(2,1)S(1)}, bf16[16,96,768]{2,1,0:T(8,128)(2,1)}, u32[]{:S(2)}, u32[]{:S(2)}) collective-permute-start(bf16[16,96,768]{2,1,0:T(8,128)(2,1)S(1)} %slice_bitcast_fusion), channel_id=1, source_target_pairs={{0,1},{1,0},{2,3},{3,2},{4,5},{5,4},{6,7},{7,6},{8,9},{9,8},{10,11... | collective-permute-start | bytes 7077896 | tf_op jit(solution)/shard_map/ppermute | solution.py:70
  203.6 15.5 %all-to-all-start.2 = ((bf16[8,32,1024]{2,1,0:T(8,128)(2,1)}), bf16[8,32,1024]{2,1,0:T(8,128)(2,1)S(1)}, u32[]{:S(2)}, u32[]{:S(2)}) async-start(bf16[8,32,1024]{2,1,0:T(8,128)(2,1)} %maximum_maximum_fusion), calls=%async_computation.2 | async-start | bytes 1048576 | tf_op jit(solution)/shard_map/all_to_all | solution.py:685
  215.8 9.2 %collective-permute-start.23 = (bf16[4,96,768]{2,1,0:T(8,128)(2,1)}, bf16[4,96,768]{2,1,0:T(8,128)(2,1)S(1)}, u32[]{:S(2)}, u32[]{:S(2)}) collective-permute-start(bf16[4,96,768]{2,1,0:T(8,128)(2,1)} %get-tuple-element.72), channel_id=1, source_target_pairs={{0,96},{1,25},{2,98},{3,27},{4,100},{5,29},{6,102},{7,31},{8,104},... | collective-permute-start | bytes 1769480 | tf_op jit(solution)/shard_map/ppermute | solution.py:63
  217.1 16.3 %collective-permute-start.22 = (bf16[4,96,768]{2,1,0:T(8,128)(2,1)S(1)}, bf16[4,96,768]{2,1,0:T(8,128)(2,1)S(1)}, u32[]{:S(2)}, u32[]{:S(2)}) collective-permute-start(bf16[4,96,768]{2,1,0:T(8,128)(2,1)S(1)} %get-tuple-element.73), channel_id=1, source_target_pairs={{0,32},{1,9},{2,34},{3,11},{4,36},{5,13},{6,38},{7,15},{8,40},{9,1... | collective-permute-start | bytes 1769480 | tf_op jit(solution)/shard_map/ppermute | solution.py:63
  217.2 16.2 %collective-permute-start.21 = (bf16[4,96,768]{2,1,0:T(8,128)(2,1)S(1)}, bf16[4,96,768]{2,1,0:T(8,128)(2,1)S(1)}, u32[]{:S(2)}, u32[]{:S(2)}) collective-permute-start(bf16[4,96,768]{2,1,0:T(8,128)(2,1)S(1)} %get-tuple-element.71), channel_id=1, source_target_pairs={{0,64},{1,17},{2,66},{3,19},{4,68},{5,21},{6,70},{7,23},{8,72},{9,... | collective-permute-start | bytes 1769480 | tf_op jit(solution)/shard_map/ppermute | solution.py:63
  243.3 12.8 %all-to-all-start.1 = ((bf16[8,12,768]{2,1,0:T(8,128)(2,1)}), bf16[8,12,768]{2,1,0:T(8,128)(2,1)S(1)}, u32[]{:S(2)}, u32[]{:S(2)}) async-start(bf16[8,12,768]{2,1,0:T(8,128)(2,1)} %copy.37), calls=%async_computation.1 | async-start | bytes 393216 | tf_op jit(solution)/shard_map/all_to_all | solution.py:596
  (40 other events, 635.6 us)

commit v2 on v1

v2 whole, which is shorter than its diff:
```python
import functools

import jax
import jax.numpy as jnp
from jax import lax
from jax.experimental import pallas as pl
from jax.experimental.pallas import tpu as pltpu
from jax.sharding import PartitionSpec as P

D = 768
NH = 24
DS = 128
HEAD = 64
CONV = 4
LEN = 256
DI = 1536
CONV_CH = 1792
NCOL = 3352
ROWS = 512
SEQS = 2
PADLEN = LEN + 8
HALF1 = 1024
WIDE1 = 2048
EPS = 1e-5
LOG2E = 1.4426950408889634
P_GAIN, P_CONV, P_BIAS, P_DT, P_RATE, P_SKIP, P_GATED, P_ROWS = 0, 1, 5, 6, 7, 8, 9, 16
LIMIT = 63 * 1024 * 1024
F32 = jnp.float32
BF16 = jnp.bfloat16
HIGHEST = lax.Precision.HIGHEST


def index_of(z, x, y, c):
    return ((z % 4 * 4 + x % 4) * 4 + y % 4) * 2 + c


def everyone():
    for z in range(4):
        for x in range(4):
            for y in range(4):
                for c in range(2):
                    yield z, x, y, c


def ring_pairs(shift, last):
    pairs = []
    for z, x, y, c in everyone():
        along_z = (c == 0) == last
        to = (z + shift, x, y, c) if along_z else (z, x + shift, y, c)
        pairs.append((index_of(z, x, y, c), index_of(*to)))
    return pairs


CORE_PAIRS = [(index_of(*p), index_of(*p[:3], 1 - p[3])) for p in everyone()]
SIXTEENS = [[k * 8 + j for k in range(16)] for j in range(8)]
EIGHTS = [[(z * 4 + x) * 8 + k for k in range(8)] for z in range(4) for x in range(4)]


def ring_gather(value, last):
    return [value] + [
        lax.ppermute(value, "fsdp", ring_pairs(shift, last)) for shift in (1, 2, 3)
    ]


def swap_core(value):
    return lax.ppermute(value, "fsdp", CORE_PAIRS)


def dot_nn(a, b):
    return jnp.dot(a, b, preferred_element_type=F32)


def dot_nt(a, b):
    return lax.dot_general(a, b, (((1,), (1,)), ((), ())), preferred_element_type=F32)


def dot_tn(a, b):
    return lax.dot_general(a, b, (((0,), (0,)), ((), ())), preferred_element_type=F32)


def dot_exact(a, b):
    return jnp.dot(a, b, preferred_element_type=F32, precision=HIGHEST)


def sigmoid(v):
    return 0.5 * jnp.tanh(0.5 * v) + 0.5


def softplus(v):
    e = jnp.exp(-jnp.abs(v))
    small = e * (1.0 - e * (0.5 - e * (1.0 / 3.0)))
    return jnp.maximum(v, 0.0) + jnp.where(e < 1e-3, small, jnp.log(1.0 + e))


def iota(shape, dim):
    return lax.broadcasted_iota(jnp.int32, shape, dim)


def source_zx(half, z0, x0, r3, r2):
    zr = jnp.where(half == 0, r3, r2)
    xr = jnp.where(half == 0, r2, r3)
    return lax.rem(z0 - zr + 4, 4) * 4 + lax.rem(x0 - xr + 4, 4)


def head_masks():
    lane = iota((1, 128), 1)
    first = jnp.where(lane < 64, 1.0, 0.0).astype(BF16)
    second = jnp.where(lane < 64, 0.0, 1.0).astype(BF16)
    return first, second


def kernel_a(
    ready, flush, pos, tokens, params,
    b0, b1, b2, b3, q0, q1, q2, q3,
    hidden_o, turned_o, w1_o, conv_in_o, slope_o, xs_o, bc, dt_pre, acum, bcum,
    hidden, turned, w1, conv_in, slope, xs, sems, out_sems, tile_sems,
):
    z0, x0, core = pos[0], pos[1], pos[2]
    copies = []
    for side, refs in enumerate(((b0, b1, b2, b3), (q0, q1, q2, q3))):
        half = core if side == 0 else 1 - core
        col = pl.multiple_of(half * HALF1, HALF1)
        for r3 in range(4):
            for r2 in range(4):
                row = pl.multiple_of(source_zx(half, z0, x0, r3, r2) * 48, 16)
                copies.append(
                    pltpu.make_async_copy(
                        refs[r3].at[pl.ds(r2 * 48, 48)],
                        w1.at[pl.ds(row, 48), pl.ds(col, HALF1)],
                        sems.at[side, r3, r2],
                    )
                )
    for copy in copies:
        copy.start()
    ready()
    gain = params[P_GAIN : P_GAIN + 1, :D]

    @pl.loop(0, ROWS // 64)
    def _(i):
        rows = pl.ds(pl.multiple_of(i * 64, 64), 64)
        t = tokens[rows].astype(F32)
        inv = lax.rsqrt(jnp.mean(t * t, axis=1, keepdims=True) + EPS)
        hidden[rows] = (t * inv * gain).astype(BF16)

    turned[...] = hidden[...].T
    for s in range(SEQS):
        conv_in[s, 0:8] = jnp.zeros((8, CONV_CH), F32)
    for copy in copies:
        copy.wait()
    outs = [
        pltpu.make_async_copy(hidden, hidden_o, out_sems.at[0]),
        pltpu.make_async_copy(w1, w1_o, out_sems.at[1]),
        pltpu.make_async_copy(turned, turned_o, out_sems.at[2]),
    ]
    for copy in outs:
        copy.start()

    def conv_tile(j, cols, emit):
        p = dot_nn(hidden[...], w1[:, cols])
        for s in range(SEQS):
            conv_in[s, 8:PADLEN, cols] = p[s * LEN : (s + 1) * LEN]
        w = params[P_CONV : P_CONV + CONV, cols]
        bias = params[P_BIAS : P_BIAS + 1, cols]
        for s in range(SEQS):

            @pl.loop(0, LEN // 32, unroll=4)
            def _(i):
                base = pl.multiple_of(i * 32, 32)
                near = conv_in[s, pl.ds(base, 40), cols]
                total = bias + w[0:1] * near[5:37]
                for k in range(1, CONV):
                    total = total + w[k : k + 1] * near[5 + k : 37 + k]
                sig = sigmoid(total)
                act = total * sig
                rows = pl.ds(pl.multiple_of(s * LEN + base, 32), 32)
                slope[rows, cols] = sig * (1.0 + total * (1.0 - sig))
                emit(rows, act.astype(BF16))

    def tile_puts(j, cols):
        puts = [
            pltpu.make_async_copy(conv_in.at[s, :, cols], conv_in_o.at[s, :, cols], tile_sems.at[j, s])
            for s in range(SEQS)
        ]
        return puts + [
            pltpu.make_async_copy(slope.at[:, cols], slope_o.at[:, cols], tile_sems.at[j, 2])
        ]

    def xs_put(j, cols):
        return pltpu.make_async_copy(xs.at[:, cols], xs_o.at[:, cols], tile_sems.at[j, 3])

    def emit_bc(rows, act):
        bc[rows] = act

    last = pl.ds(1536, 256)
    conv_tile(6, last, emit_bc)
    for put in tile_puts(6, last):
        put.start()

    pre = dot_nn(hidden[...], w1[:, CONV_CH : CONV_CH + 128]) + params[P_DT : P_DT + 1, :128]
    dt_pre[...] = pre
    step = softplus(pre)
    inc = step * params[P_RATE : P_RATE + 1, :128] * LOG2E
    log_step = jnp.log(jnp.maximum(step, 1e-37)) * LOG2E
    lower = jnp.where(iota((LEN, LEN), 0) >= iota((LEN, LEN), 1), 1.0, 0.0)
    for s in range(SEQS):
        rows = slice(s * LEN, (s + 1) * LEN)
        a = dot_exact(lower, inc[rows])
        acum[rows] = a
        bcum[rows] = a - log_step[rows]
    flush()

    @pl.loop(0, 6)
    def _(j):
        cols = pl.ds(pl.multiple_of(j * 256, 256), 256)

        def emit(rows, act):
            xs[rows, cols] = act

        conv_tile(j, cols, emit)
        for put in tile_puts(j, cols) + [xs_put(j, cols)]:
            put.start()

    @pl.loop(0, 6)
    def _(j):
        cols = pl.ds(pl.multiple_of(j * 256, 256), 256)
        for put in tile_puts(j, cols) + [xs_put(j, cols)]:
            put.wait()

    for put in tile_puts(6, last) + outs:
        put.wait()


def kernel_s(ready, flush, params, xs_i, bc, acum, bcum, y_o, xs, y, score, bcum_t, in_sems, out_sems):
    gets = [
        pltpu.make_async_copy(xs_i.at[pl.ds(s * LEN, LEN)], xs.at[pl.ds(s * LEN, LEN)], in_sems.at[s])
        for s in range(SEQS)
    ]
    for copy in gets:
        copy.start()
    below = iota((LEN, LEN), 0) >= iota((LEN, LEN), 1)
    mask0, mask1 = head_masks()
    outs = []
    ready()
    for s in range(SEQS):
        rows = slice(s * LEN, (s + 1) * LEN)
        a = acum[rows]
        bcum_t[...] = bcum[rows].T
        score[...] = jnp.where(below, dot_nt(bc[rows, DS:], bc[rows, :DS]), 0.0)
        gets[s].wait()

        @pl.loop(0, NH // 2, unroll=4)
        def _(p):
            lanes = pl.ds(pl.multiple_of(p * 128, 128), 128)
            x = xs[s * LEN : (s + 1) * LEN, lanes]
            turned = pltpu.roll(a, lax.rem(128 - 2 * p, 128), 1)
            top = jnp.zeros((128, 128), F32)
            low = jnp.zeros((128, 128), F32)
            for i, mask in enumerate((mask0, mask1)):
                col = turned[:, i : i + 1]
                row = bcum_t[pl.ds(2 * p + i, 1), :]
                xm = x * mask
                e0 = jnp.exp2(jnp.minimum(col[:128] - row[:, :128], 64.0))
                m0 = (e0 * score[:128, :128]).astype(BF16)
                top = top + dot_nn(m0, xm[:128])
                e1 = jnp.exp2(jnp.minimum(col[128:] - row, 64.0))
                m1 = (e1 * score[128:, :]).astype(BF16)
                low = low + dot_nn(m1, xm)
            skip = params[P_SKIP : P_SKIP + 1, lanes]
            y[s * LEN : s * LEN + 128, lanes] = top + skip * x[:128].astype(F32)
            y[s * LEN + 128 : (s + 1) * LEN, lanes] = low + skip * x[128:].astype(F32)

        span = pl.ds(s * LEN, LEN)
        outs.append(pltpu.make_async_copy(y.at[span], y_o.at[span], out_sems.at[s]))
        outs[-1].start()
    for copy in outs:
        copy.wait()


def store_gate(turned, big, dest, extra):
    @pl.loop(0, 3)
    def _(j):
        cols = pl.ds(pl.multiple_of(j * 256, 256), 256)
        for lr in range(2):
            src = pl.ds(pl.multiple_of(j * 256 + lr * D, 256), 256)
            g = dot_nn(turned[...], big[:, src])
            for zx in range(16):
                part = g[zx * 48 : zx * 48 + 48]
                if extra is not None:
                    part = part + extra[zx, lr * 48 : lr * 48 + 48, cols].astype(F32)
                dest[zx, lr * 48 : lr * 48 + 48, cols] = part.astype(BF16)


def store_out(small, big, dest, extra):
    for t in range(4):
        g = dot_tn(big[:, t * 384 : (t + 1) * 384], small[...])
        for k in range(4):
            part = g[k * 96 : (k + 1) * 96]
            if extra is not None:
                part = part + extra[t * 4 + k].astype(F32)
            dest[t * 4 + k] = part.astype(BF16)


def kernel_b(
    ready, flush, pos, hidden, turned, y_i, tokens_i, cot_i, params,
    b0, b1, b2, b3, q0, q1, q2, q3,
    out_o, d_y_o, grads_o, d_hid_o, normed_o, d_gate_o, gain_grad,
    y, tokens, cot, out, d_y, grads, d_hid,
    weights, gate_in, d_normed, normed, d_gate, gate_inv, acc, sems, io_sems,
):
    core = pos[2]
    z0, x0 = pos[0], pos[1]
    copies = ([], [])
    for side, refs in enumerate(((b0, b1, b2, b3), (q0, q1, q2, q3))):
        half = core if side == 0 else 1 - core
        for r3 in range(4):
            for r2 in range(4):
                zx = source_zx(half, z0, x0, r3, r2)
                for lr in range(2):
                    row = jnp.where(half == 0, lr * D + zx * 48, DI + zx * 96 + lr * 48)
                    copies[side].append(
                        pltpu.make_async_copy(
                            refs[r3].at[pl.ds(r2 * 96 + lr * 48, 48)],
                            weights.at[pl.ds(pl.multiple_of(row, 16), 48)],
                            sems.at[side, r3, r2, lr],
                        )
                    )

    def each(side, act):
        @pl.when(core == side)
        def _():
            for copy in copies[0]:
                act(copy)

        @pl.when(core != side)
        def _():
            for copy in copies[1]:
                act(copy)

    get_y = pltpu.make_async_copy(y_i, y, io_sems.at[0])
    get_tokens = pltpu.make_async_copy(tokens_i, tokens, io_sems.at[1])
    get_cot = pltpu.make_async_copy(cot_i, cot, io_sems.at[2])
    put_out = pltpu.make_async_copy(out, out_o, io_sems.at[3])
    put_dy = pltpu.make_async_copy(d_y, d_y_o, io_sems.at[4])
    put_dhid = pltpu.make_async_copy(d_hid, d_hid_o, io_sems.at[5])
    each(0, lambda copy: copy.start())
    get_y.start()
    each(1, lambda copy: copy.start())
    get_tokens.start()
    get_cot.start()
    ready()
    gain = params[P_GATED : P_GATED + 1, :DI]
    each(0, lambda copy: copy.wait())

    @pl.loop(0, 3)
    def _(j):
        cols = pl.ds(pl.multiple_of(j * 256, 256), 256)
        right = pl.ds(pl.multiple_of(j * 256 + D, 256), 256)
        gate_in[:, cols] = dot_nn(hidden[...], weights[0:D, cols])
        gate_in[:, right] = dot_nn(hidden[...], weights[D:DI, cols])

    get_y.wait()

    @pl.loop(0, ROWS // 16, unroll=4)
    def _(i):
        rows = pl.ds(pl.multiple_of(i * 16, 16), 16)
        g = gate_in[rows]
        gated = y[rows] * (g * sigmoid(g))
        inv = lax.rsqrt(jnp.mean(gated * gated, axis=1, keepdims=True) + EPS)
        gate_inv[rows] = jnp.broadcast_to(inv, (16, 128))
        normed[rows] = (gated * inv * gain).astype(BF16)

    put_normed = pltpu.make_async_copy(normed, normed_o, io_sems.at[6])
    put_normed.start()
    each(1, lambda copy: copy.wait())
    get_tokens.wait()
    get_cot.wait()

    @pl.loop(0, 3)
    def _(j):
        cols = pl.ds(pl.multiple_of(j * 256, 256), 256)
        mixed = dot_nn(normed[...], weights[DI:, cols])
        out[:, cols] = (tokens[:, cols].astype(F32) + mixed).astype(BF16)

    put_out.start()

    @pl.loop(0, 6)
    def _(j):
        cols = pl.ds(pl.multiple_of(j * 256, 256), 256)
        d_normed[:, cols] = dot_nt(cot[...], weights[pl.ds(pl.multiple_of(j * 256 + DI, 256), 256)])

    acc[...] = jnp.zeros_like(acc)

    @pl.loop(0, ROWS // 16, unroll=4)
    def _(i):
        rows = pl.ds(pl.multiple_of(i * 16, 16), 16)
        g = gate_in[rows]
        sig = sigmoid(g)
        act = g * sig
        yv = y[rows]
        inv = gate_inv[rows][:, 0:1]
        gnorm = yv * act * inv
        dn = d_normed[rows]
        prod = dn * gnorm
        acc[...] += prod
        dgn = dn * gain
        mean = jnp.mean(dgn * gnorm, axis=1, keepdims=True)
        d_gated = inv * (dgn - gnorm * mean)
        d_y[rows] = d_gated * act
        d_gate[rows] = (d_gated * yv * (sig * (1.0 + g * (1.0 - sig)))).astype(BF16)

    put_dy.start()
    put_gate = pltpu.make_async_copy(d_gate, d_gate_o, io_sems.at[7])
    put_gate.start()
    gain_grad[...] = jnp.sum(acc[...], axis=0, keepdims=True)
    flush()

    @pl.when(core == 0)
    def _():
        store_out(cot, normed, grads, None)

    @pl.when(core != 0)
    def _():
        store_gate(turned, d_gate, grads, None)

    put_grads = pltpu.make_async_copy(grads, grads_o, io_sems.at[8])
    put_grads.start()

    @pl.loop(0, 3)
    def _(j):
        cols = pl.ds(pl.multiple_of(j * 256, 256), 256)
        right = pl.ds(pl.multiple_of(j * 256 + D, 256), 256)
        d_hid[:, cols] = dot_nt(d_gate[:, :D], weights[cols]) + dot_nt(
            d_gate[:, D:], weights[right]
        )

    put_dhid.start()
    for copy in (put_out, put_dy, put_normed, put_gate, put_grads, put_dhid):
        copy.wait()


def kernel_f(ready, _, pos, turned_i, cot_i, d_gate, normed, got, total_o, turned, cot, big, total, sems):
    core = pos[2]

    @pl.when(core == 0)
    def _():
        gets = [
            pltpu.make_async_copy(turned_i, turned, sems.at[0]),
            pltpu.make_async_copy(d_gate, big, sems.at[1]),
        ]
        for get in gets:
            get.start()
        for get in gets:
            get.wait()
        ready()
        store_gate(turned, big, total, got)

    @pl.when(core != 0)
    def _():
        gets = [
            pltpu.make_async_copy(cot_i, cot, sems.at[0]),
            pltpu.make_async_copy(normed, big, sems.at[1]),
        ]
        for get in gets:
            get.start()
        for get in gets:
            get.wait()
        ready()
        store_out(cot, big, total, got)

    put = pltpu.make_async_copy(total, total_o, sems.at[2])
    put.start()
    put.wait()


def split_dot(v, pick):
    hi = v.astype(BF16)
    lo = (v - hi.astype(F32)).astype(BF16)
    return dot_nn(jnp.concatenate([hi, lo], axis=1), pick)


def kernel_c(
    ready, flush, xs_i, bc, acum, bcum, dt_pre, d_y_i, y_i, params,
    d_act_o, d_pre_o, g_skip, g_dt, g_alog,
    xs, d_y, y, d_act, score_t, acum_t, d_score, rsum, csum, in_sems, out_sems,
):
    gets = [
        [
            pltpu.make_async_copy(
                src.at[pl.ds(s * LEN, LEN)], dst.at[pl.ds(s * LEN, LEN)], in_sems.at[s, k]
            )
            for k, (src, dst) in enumerate(((xs_i, xs), (d_y_i, d_y), (y_i, y)))
        ]
        for s in range(SEQS)
    ]
    for copy in gets[0] + gets[1]:
        copy.start()
    above = iota((LEN, LEN), 0) <= iota((LEN, LEN), 1)
    upper = jnp.where(above, 1.0, 0.0)
    mask0, mask1 = head_masks()
    lane_head = iota((256, 128), 0) % 128 // 64
    head_col = iota((256, 128), 1)
    lane = iota((1, 128), 1)
    g_skip[...] = jnp.zeros_like(g_skip)
    g_dt[...] = jnp.zeros_like(g_dt)
    g_alog[...] = jnp.zeros_like(g_alog)
    ready()
    rate = params[P_RATE : P_RATE + 1, :128]
    puts = []
    for s in range(SEQS):
        rows = pl.ds(s * LEN, LEN)
        acum_t[...] = acum[rows].T
        score_t[...] = jnp.where(above, dot_nt(bc[rows, :DS], bc[rows, DS:]), 0.0)
        d_score[...] = jnp.zeros_like(d_score)
        rsum[...] = jnp.zeros_like(rsum)
        csum[...] = jnp.zeros_like(csum)
        b = bcum[rows]
        for copy in gets[s]:
            copy.wait()

        @pl.loop(0, NH // 2, unroll=4)
        def _(p):
            lanes = pl.ds(pl.multiple_of(p * 128, 128), 128)
            x = xs[rows, lanes]
            dy = d_y[rows, lanes]
            ds = dy.astype(BF16)
            turned = pltpu.roll(b, lax.rem(128 - 2 * p, 128), 1)
            top = jnp.zeros((128, 128), F32)
            low = jnp.zeros((128, 128), F32)
            for i, mask in enumerate((mask0, mask1)):
                col = turned[:, i : i + 1]
                row = acum_t[pl.ds(2 * p + i, 1), :]
                dm = ds * mask
                xm = x * mask
                e0 = jnp.exp2(jnp.minimum(row - col[:128], 64.0))
                m0 = (e0 * score_t[:128, :]).astype(BF16)
                top = top + dot_nn(m0, dm)
                d_score[:128, :] += dot_nt(xm[:128], ds) * e0
                e1 = jnp.exp2(jnp.minimum(row[:, 128:] - col[128:], 64.0))
                m1 = (e1 * score_t[128:, 128:]).astype(BF16)
                low = low + dot_nn(m1, dm[128:])
                d_score[128:, 128:] += dot_nt(xm[128:], ds[128:]) * e1
            dxs = jnp.concatenate([top, low], axis=0)
            skip = params[P_SKIP : P_SKIP + 1, lanes]
            xf = x.astype(F32)
            own = ds.astype(F32) * (y[rows, lanes] - skip * xf)
            across = xf * dxs
            pick = jnp.where(lane_head + 2 * p == head_col, 1.0, 0.0).astype(BF16)
            rsum[...] += split_dot(own, pick)
            csum[...] += split_dot(across, pick)
            both = jnp.sum(dy * xf, axis=0, keepdims=True)
            first = jnp.sum(jnp.where(lane < 64, both, 0.0), axis=1, keepdims=True)
            second = jnp.sum(jnp.where(lane < 64, 0.0, both), axis=1, keepdims=True)
            g_skip[...] += jnp.where(lane == 2 * p, first, 0.0) + jnp.where(
                lane == 2 * p + 1, second, 0.0
            )
            d_act[rows, lanes] = skip * dy + dxs

        pre = dt_pre[rows]
        step = softplus(pre)
        sig = 1.0 / (1.0 + jnp.exp(-pre))
        ratio = jnp.where(pre < -20.0, 1.0, sig / jnp.maximum(step, 1e-30))
        d_cum = rsum[...] - csum[...]
        d_inc = dot_exact(upper, d_cum)
        g_alog[...] += jnp.sum(d_inc * step, axis=0, keepdims=True) * rate
        d_pre = csum[...] * ratio + d_inc * rate * sig
        g_dt[...] += jnp.sum(d_pre, axis=0, keepdims=True)
        d_pre_o[rows] = d_pre.astype(BF16)
        dsc = jnp.where(above, d_score[...], 0.0).astype(BF16)
        d_act[rows, DI : DI + DS] = dot_nn(dsc, bc[rows, DS:])
        d_act[rows, DI + DS :] = dot_tn(dsc, bc[rows, :DS])
        puts.append(pltpu.make_async_copy(d_act.at[rows], d_act_o.at[rows], out_sems.at[s]))
        puts[-1].start()
    flush()
    for put in puts:
        put.wait()


def kernel_e(
    ready, flush, pos, act_i, d_pre, conv_in_i, slope_i, params, turned, _,
    grads_o, d_proj_o, g_conv_w, g_conv_b,
    d_proj, d_act, slope, conv_in, grads, sems, out_sems, proj_sems,
):
    core = pos[2]

    def tile_copies(j):
        cols = pl.ds(pl.multiple_of(j * 256, 256), 256)
        pairs = []
        for s in range(SEQS):
            pairs.append((act_i.at[pl.ds(s * LEN, LEN), cols], d_act.at[s, 0:LEN, cols]))
            pairs.append((slope_i.at[pl.ds(s * LEN, LEN), cols], slope.at[s, 0:LEN, cols]))
            pairs.append((conv_in_i.at[s, :, cols], conv_in.at[s, :, cols]))
        return [
            pltpu.make_async_copy(src, dst, sems.at[j, k]) for k, (src, dst) in enumerate(pairs)
        ]

    for j in range(CONV_CH // 256):
        for copy in tile_copies(j):
            copy.start()
    for s in range(SEQS):
        d_act[s, LEN:] = jnp.zeros((8, CONV_CH), F32)
        slope[s, LEN:] = jnp.zeros((8, CONV_CH), F32)
    ready()
    d_proj[:, CONV_CH : CONV_CH + 128] = d_pre[...]
    d_proj[:, CONV_CH + 128 :] = jnp.zeros((ROWS, 128), BF16)

    def put_tile(j):
        cols = pl.ds(pl.multiple_of(j * 256, 256), 256)
        return pltpu.make_async_copy(d_proj.at[:, cols], d_proj_o.at[:, cols], proj_sems.at[j])

    put_tile(7).start()

    @pl.loop(0, CONV_CH // 256)
    def _(j):
        cols = pl.ds(pl.multiple_of(j * 256, 256), 256)
        for copy in tile_copies(j):
            copy.wait()
        w = params[P_CONV : P_CONV + CONV, cols]
        zero = jnp.zeros((8, 256), F32)
        sums = (zero,) * (CONV + 1)
        for s in range(SEQS):

            def chunk(i, sums):
                base = pl.multiple_of(i * 32, 32)
                later = d_act[s, pl.ds(base, 40), cols] * slope[s, pl.ds(base, 40), cols]
                near = conv_in[s, pl.ds(base, 40), cols]
                here = later[0:32]
                back = w[CONV - 1 : CONV] * here
                for k in range(CONV - 1):
                    back = back + w[k : k + 1] * later[3 - k : 35 - k]
                d_proj[pl.ds(pl.multiple_of(s * LEN + base, 32), 32), cols] = back.astype(BF16)

                def fold(v):
                    return (v[0:8] + v[8:16]) + (v[16:24] + v[24:32])

                new = [sums[k] + fold(here * near[5 + k : 37 + k]) for k in range(CONV)]
                return tuple(new) + (sums[CONV] + fold(here),)

            sums = lax.fori_loop(0, LEN // 32, chunk, sums, unroll=4)
        for k in range(CONV):
            g_conv_w[k : k + 1, cols] = jnp.sum(sums[k], axis=0, keepdims=True)
        g_conv_b[:, cols] = jnp.sum(sums[CONV], axis=0, keepdims=True)
        put_tile(j).start()

    flush()

    def put_grads(j):
        cols = pl.ds(pl.multiple_of(j * 256, 256), 256)
        return pltpu.make_async_copy(grads.at[:, cols], grads_o.at[:, cols], out_sems.at[j])

    @pl.loop(0, 4)
    def _(j):
        cols = pl.ds(pl.multiple_of(j * 256, 256), 256)
        src = pl.ds(pl.multiple_of(j * 256 + (1 - core) * HALF1, 256), 256)
        grads[:, cols] = dot_nn(turned[...], d_proj[:, src]).astype(BF16)
        put_grads(j).start()

    for j in range(8):
        put_tile(j).wait()
    for j in range(4):
        put_grads(j).wait()


def kernel_g(
    ready, _, pos, turned, d_proj_i, got, g_conv_w, g_conv_b, g_gated, g_norm,
    g_dt, g_alog, g_skip, __, out0, out1, out2, out3,
    total, d_proj, small, sem, out_sems,
):
    z0, x0, core = pos[0], pos[1], pos[2]
    src = pl.ds(pl.multiple_of(core * HALF1, HALF1), HALF1)
    get = pltpu.make_async_copy(d_proj_i.at[:, src], d_proj, sem)
    get.start()
    rest = CONV_CH - HALF1
    small[...] = jnp.zeros_like(small)
    ready()
    small[0:4] = g_conv_w[:, :HALF1]
    small[4:8, :rest] = g_conv_w[:, HALF1:]
    small[8:9] = g_conv_b[:, :HALF1]
    small[9:10, :rest] = g_conv_b[:, HALF1:]
    small[10:11] = g_gated[:, :HALF1]
    small[11:12, : DI - HALF1] = g_gated[:, HALF1:]
    small[12:13, :D] = g_norm[...]
    small[12:13, D : D + 128] = g_dt[...]
    small[12:13, D + 128 :] = g_alog[...]
    small[14:15, :128] = g_skip[...]
    for k in (12, 14):
        exact = small[k : k + 1]
        small[k + 1 : k + 2] = exact - exact.astype(BF16).astype(F32)
    sent = small[...].astype(BF16)
    for r3 in range(4):
        total[r3, 192:208] = sent
    get.wait()

    @pl.loop(0, 4)
    def _(j):
        cols = pl.ds(pl.multiple_of(j * 256, 256), 256)
        g = dot_nn(turned[...], d_proj[:, cols]) + got[:, cols].astype(F32)
        g = g.astype(BF16)
        for zx in range(16):
            dz = lax.rem(zx // 4 - z0 + 4, 4)
            dx = lax.rem(zx % 4 - x0 + 4, 4)
            r3 = jnp.where(core == 0, dz, dx)
            r2 = jnp.where(core == 0, dx, dz)
            rows = pl.ds(pl.multiple_of(r2 * 48, 16), 48)
            total[r3, rows, cols] = g[zx * 48 : zx * 48 + 48]

    puts = [
        pltpu.make_async_copy(total.at[r], out, out_sems.at[r])
        for r, out in enumerate((out0, out1, out2, out3))
    ]
    for put in puts:
        put.start()
    for put in puts:
        put.wait()


def sum_of_four(a, b, c, d):
    return (a[...].astype(F32) + c[...].astype(F32)) + (b[...].astype(F32) + d[...].astype(F32))


def kernel_k(ready, flush, own, got1, got2, got3, *outs):
    ready()
    total = sum_of_four(own, got1, got2, got3).astype(BF16)
    for r2, out in enumerate(outs):
        out[0:48] = total[r2 * 48 : r2 * 48 + 48]
        out[48:64] = total[192:208]
    flush()


def kernel_l(ready, flush, own, got1, got2, got3, two, out):
    ready()
    total = sum_of_four(own, got1, got2, got3)
    rides = jnp.concatenate([total[48:56], total[56:64]], axis=1).astype(BF16)
    zero = jnp.zeros((2, HALF1), F32)
    for d in range(8):
        eight = slice(d * 8, d * 8 + 8)
        out[eight, :DI] = two[eight]
        piece = jnp.concatenate([total[d * 6 : d * 6 + 6], zero], axis=0)
        out[eight, DI : DI + HALF1] = piece.astype(BF16)
        out[eight, DI + HALF1 :] = rides
    flush()


def kernel_d(
    ready, flush, d_proj_i, w1_i, d_hid_i, tokens_i, params, cot_i, grad_tokens_o, gain_grad,
    d_proj, w1, d_hid, tokens, cot, d_full, grad_tokens, sems, out_sems,
):
    gets = [
        pltpu.make_async_copy(src, dst, sems.at[k])
        for k, (src, dst) in enumerate(
            (
                (w1_i, w1), (d_proj_i, d_proj), (d_hid_i, d_hid),
                (tokens_i, tokens), (cot_i, cot),
            )
        )
    ]
    for copy in gets:
        copy.start()
    for copy in gets[:3]:
        copy.wait()

    @pl.loop(0, 3)
    def _(j):
        cols = pl.ds(pl.multiple_of(j * 256, 256), 256)
        d_full[:, cols] = d_hid[:, cols] + dot_nt(d_proj[...], w1[cols])

    gets[3].wait()
    gets[4].wait()
    ready()
    gain = params[P_GAIN : P_GAIN + 1, :D]

    def chunk(i, total):
        rows = pl.ds(pl.multiple_of(i * 32, 32), 32)
        t = tokens[rows].astype(F32)
        inv = lax.rsqrt(jnp.mean(t * t, axis=1, keepdims=True) + EPS)
        normal = t * inv
        dh = d_full[rows]
        prod = dh * normal
        dn = dh * gain
        mean = jnp.mean(dn * normal, axis=1, keepdims=True)
        grad_tokens[rows] = cot[rows].astype(F32) + inv * (dn - normal * mean)
        return total + (prod[0:8] + prod[8:16]) + (prod[16:24] + prod[24:32])

    total = jnp.zeros((8, D), F32)
    puts = []
    for s in range(SEQS):
        total = lax.fori_loop(s * LEN // 32, (s + 1) * LEN // 32, chunk, total, unroll=4)
        span = pl.ds(s * LEN, LEN)
        puts.append(
            pltpu.make_async_copy(grad_tokens.at[span], grad_tokens_o.at[span], out_sems.at[s])
        )
        puts[-1].start()
    gain_grad[...] = jnp.sum(total, axis=0, keepdims=True)
    flush()
    for put in puts:
        put.wait()


def kernel_h(
    ready, flush, got, g_in, g_out, g_norm, g_conv_w, g_conv_b, g_dt, g_alog, g_skip, g_gated, rows,
):
    def added(core, start, size):
        parts = [
            got[16 * y + 8 * core : 16 * y + 8 * core + 8, start : start + size].astype(F32)
            for y in range(4)
        ]
        return (parts[0] + parts[1]) + (parts[2] + parts[3])

    ready()
    rows[:, :DI] = added(0, 0, DI)
    rows[:, DI : DI + HALF1] = added(0, DI, HALF1)
    rows[:, DI + HALF1 :] = added(1, DI, HALF1)
    outs = added(1, 0, DI)
    for r in range(6):
        g_in[pl.ds(r * NCOL, NCOL)] = rows[r : r + 1, :NCOL].reshape(NCOL)
        g_out[pl.ds(r * DI, DI)] = outs[r : r + 1].reshape(DI)
    base = DI + HALF1
    top = added(0, base, HALF1) + added(1, base, HALF1)
    low = added(0, base + HALF1, HALF1) + added(1, base + HALF1, HALF1)
    rest = CONV_CH - HALF1
    g_conv_w[:, :HALF1] = top[0:4]
    g_conv_w[:, HALF1:] = top[4:8, :rest]
    g_conv_b[...] = jnp.concatenate([low[0:1], low[1:2, :rest]], axis=1).reshape(CONV_CH)
    g_gated[...] = jnp.concatenate([low[2:3], low[3:4, : DI - HALF1]], axis=1).reshape(DI)
    exact = low[4:5] + low[5:6]
    skip = low[6:7, :128] + low[7:8, :128]
    g_norm[...] = exact[:, :D].reshape(D)
    g_dt[...] = exact[0, D : D + NH]
    g_alog[...] = exact[0, D + 128 : D + 128 + NH]
    g_skip[...] = skip[0, :NH]
    flush()


VM = pl.BlockSpec(memory_space=pltpu.VMEM)
SM = pl.BlockSpec(memory_space=pltpu.SMEM)
HB = pl.BlockSpec(memory_space=pl.ANY)


def call(kernel, name, ins, outs, scratch, args, us=0.01):
    taken = [k for k, spec in enumerate(ins) if spec is VM]
    given = [k for k, out in enumerate(outs) if out[2] is VM]
    n_in, n_out, n_scratch = len(ins), len(outs), len(scratch)

    def body(*refs):
        in_refs = list(refs[:n_in])
        out_refs = list(refs[n_in : n_in + n_out])
        own = refs[n_in + n_out : n_in + n_out + n_scratch]
        rest = refs[n_in + n_out + n_scratch :]
        in_bufs, rest = rest[: len(taken)], rest[len(taken) :]
        out_bufs, rest = rest[: len(given)], rest[len(given) :]
        gets, puts = [], []
        for n, k in enumerate(taken):
            gets.append(pltpu.make_async_copy(in_refs[k], in_bufs[n], rest[0].at[n]))
            in_refs[k] = in_bufs[n]
        for n, k in enumerate(given):
            puts.append(pltpu.make_async_copy(out_bufs[n], out_refs[k], rest[1].at[n]))
            out_refs[k] = out_bufs[n]
        for copy in gets:
            copy.start()

        def ready():
            for copy in gets:
                copy.wait()

        def flush():
            for copy in puts:
                copy.start()

        kernel(ready, flush, *in_refs, *out_refs, *own)
        for copy in puts:
            copy.wait()

    dma = pltpu.SemaphoreType.DMA
    extra = [pltpu.VMEM(args[k].shape, args[k].dtype) for k in taken]
    extra += [pltpu.VMEM(outs[k][0], outs[k][1]) for k in given]
    extra += [dma((max(len(taken), 1),)), dma((max(len(given), 1),))]
    return pl.pallas_call(
        body,
        name=name,
        in_specs=[HB if spec is VM else spec for spec in ins],
        out_specs=[HB] * n_out,
        out_shape=[jax.ShapeDtypeStruct(o[0], o[1]) for o in outs],
        scratch_shapes=list(scratch) + extra,
        compiler_params=pltpu.CompilerParams(vmem_limit_bytes=LIMIT),
        cost_estimate=pl.CostEstimate(
            flops=int(us * 1.1e9), bytes_accessed=100_000, transcendentals=0
        ),
    )(*args)


def per_device(
    tokens,
    in_weight,
    out_weight,
    norm_gain,
    conv_weight,
    conv_bias,
    dt_bias,
    a_log,
    d_skip,
    gated_gain,
    cotangent,
):
    me = lax.axis_index("fsdp")
    core = lax.rem(me, 2)
    pos = jnp.stack([me // 32, lax.rem(me // 8, 4), core]).astype(jnp.int32)

    win = in_weight.reshape(6, NCOL)
    conv_cols = jnp.pad(win[:, DI:], ((0, 0), (0, WIDE1 - (NCOL - DI))))
    halves = jnp.stack(
        [
            jnp.concatenate([conv_cols[:, :HALF1], win[:, :DI]], axis=1),
            jnp.concatenate([conv_cols[:, HALF1:], out_weight.reshape(6, DI)], axis=1),
        ]
    )
    sent = jnp.broadcast_to(halves[None], (4, 2, 6, HALF1 + DI)).reshape(8, 6, HALF1 + DI)
    eight = lax.all_to_all(sent, "fsdp", 0, 0, axis_index_groups=EIGHTS)

    def row(v):
        return jnp.pad(v, (0, CONV_CH - v.shape[0]))[None]

    params = jnp.concatenate(
        [
            row(norm_gain), conv_weight, row(conv_bias), row(dt_bias), row(-jnp.exp(a_log)),
            row(jnp.repeat(d_skip, HEAD)), row(gated_gain),
            jnp.zeros((P_ROWS - P_GATED - 1, CONV_CH), F32),
        ],
        axis=0,
    )
    eight, params, pos = lax.optimization_barrier((eight, params, pos))
    near = ring_gather(eight.reshape(48, HALF1 + DI), False)
    own1 = ring_gather(jnp.concatenate([v[:, :HALF1] for v in near], axis=0), True)

    def second_part(v):
        as_gate = jnp.concatenate([v[:, HALF1 : HALF1 + D], v[:, HALF1 + D :]], axis=0)
        return jnp.where(core == 0, as_gate, v[:, HALF1:].reshape(96, D))

    near2 = jnp.concatenate([second_part(v) for v in near], axis=0)
    own1, near2 = lax.optimization_barrier((own1, near2))
    other1 = [swap_core(v) for v in own1]
    own2 = ring_gather(near2, True)
    dma = pltpu.SemaphoreType.DMA

    hidden, turned, w1, conv_in, slope, xs, bc, dt_pre, acum, bcum = call(
        kernel_a,
        "forward_conv",
        [SM] + [VM] * 2 + [HB] * 8,
        [
            ((ROWS, D), BF16, HB),
            ((D, ROWS), BF16, HB),
            ((D, WIDE1), BF16, HB),
            ((SEQS, PADLEN, CONV_CH), F32, HB),
            ((ROWS, CONV_CH), F32, HB),
            ((ROWS, DI), BF16, HB),
            ((ROWS, 2 * DS), BF16, VM),
            ((ROWS, 128), F32, VM),
            ((ROWS, 128), F32, VM),
            ((ROWS, 128), F32, VM),
        ],
        [
            pltpu.VMEM((ROWS, D), BF16),
            pltpu.VMEM((D, ROWS), BF16),
            pltpu.VMEM((D, WIDE1), BF16),
            pltpu.VMEM((SEQS, PADLEN, CONV_CH), F32),
            pltpu.VMEM((ROWS, CONV_CH), F32),
            pltpu.VMEM((ROWS, DI), BF16),
            dma((2, 4, 4)),
            dma((3,)),
            dma((7, 4)),
        ],
        [pos, tokens, params] + own1 + other1,
        14,
    )
    other2 = [swap_core(v) for v in own2]
    (y,) = call(
        kernel_s,
        "forward_ssd",
        [VM, HB, VM, VM, VM],
        [((ROWS, DI), F32, HB)],
        [
            pltpu.VMEM((ROWS, DI), BF16),
            pltpu.VMEM((ROWS, DI), F32),
            pltpu.VMEM((LEN, LEN), F32),
            pltpu.VMEM((128, LEN), F32),
            dma((2,)),
            dma((2,)),
        ],
        [params, xs, bc, acum, bcum],
        9,
    )

    out, d_y, grads2, d_hid, normed, d_gate, g_gated = call(
        kernel_b,
        "gate_output",
        [SM, VM, VM, HB, HB, HB, VM] + [HB] * 8,
        [
            ((ROWS, D), BF16, HB),
            ((ROWS, DI), F32, HB),
            ((16, 96, D), BF16, HB),
            ((ROWS, D), F32, HB),
            ((ROWS, DI), BF16, HB),
            ((ROWS, DI), BF16, HB),
            ((1, DI), F32, VM),
        ],
        [
            pltpu.VMEM((ROWS, DI), F32),
            pltpu.VMEM((ROWS, D), BF16),
            pltpu.VMEM((ROWS, D), BF16),
            pltpu.VMEM((ROWS, D), BF16),
            pltpu.VMEM((ROWS, DI), F32),
            pltpu.VMEM((16, 96, D), BF16),
            pltpu.VMEM((ROWS, D), F32),
            pltpu.VMEM((2 * DI, D), BF16),
            pltpu.VMEM((ROWS, DI), F32),
            pltpu.VMEM((ROWS, DI), F32),
            pltpu.VMEM((ROWS, DI), BF16),
            pltpu.VMEM((ROWS, DI), BF16),
            pltpu.VMEM((ROWS, 128), F32),
            pltpu.VMEM((16, DI), F32),
            dma((2, 4, 4, 2)),
            dma((9,)),
        ],
        [pos, hidden, turned, y, tokens, cotangent, params] + own2 + other2,
        18,
    )

    got2 = swap_core(grads2)
    d_act, d_pre, g_skip, g_dt, g_alog = call(
        kernel_c,
        "backward_ssd",
        [HB, VM, VM, VM, VM, HB, HB, VM],
        [
            ((ROWS, CONV_CH), F32, HB),
            ((ROWS, 128), BF16, VM),
            ((1, 128), F32, VM),
            ((1, 128), F32, VM),
            ((1, 128), F32, VM),
        ],
        [
            pltpu.VMEM((ROWS, DI), BF16),
            pltpu.VMEM((ROWS, DI), F32),
            pltpu.VMEM((ROWS, DI), F32),
            pltpu.VMEM((ROWS, CONV_CH), F32),
            pltpu.VMEM((LEN, LEN), F32),
            pltpu.VMEM((128, LEN), F32),
            pltpu.VMEM((LEN, LEN), F32),
            pltpu.VMEM((LEN, 128), F32),
            pltpu.VMEM((LEN, 128), F32),
            dma((2, 3)),
            dma((2,)),
        ],
        [xs, bc, acum, bcum, dt_pre, d_y, y, params],
        14,
    )

    (sum2,) = call(
        kernel_f,
        "grad_gate_out",
        [SM, HB, HB, HB, HB, VM],
        [((16, 96, D), BF16, HB)],
        [
            pltpu.VMEM((D, ROWS), BF16),
            pltpu.VMEM((ROWS, D), BF16),
            pltpu.VMEM((ROWS, DI), BF16),
            pltpu.VMEM((16, 96, D), BF16),
            dma((3,)),
        ],
        [pos, turned, cotangent, d_gate, normed, got2],
    )
    before = sum2
    sum2 = lax.all_to_all(sum2, "fsdp", 0, 0, axis_index_groups=SIXTEENS)

    grads1, d_proj, g_conv_w, g_conv_b = call(
        kernel_e,
        "backward_conv",
        [SM, HB, VM, HB, HB, VM, VM, HB],
        [
            ((D, HALF1), BF16, HB),
            ((ROWS, WIDE1), BF16, HB),
            ((CONV, CONV_CH), F32, VM),
            ((1, CONV_CH), F32, VM),
        ],
        [
            pltpu.VMEM((ROWS, WIDE1), BF16),
            pltpu.VMEM((SEQS, PADLEN, CONV_CH), F32),
            pltpu.VMEM((SEQS, PADLEN, CONV_CH), F32),
            pltpu.VMEM((SEQS, PADLEN, CONV_CH), F32),
            pltpu.VMEM((D, HALF1), BF16),
            dma((7, 6)),
            dma((4,)),
            dma((8,)),
        ],
        [pos, d_act, d_pre, conv_in, slope, params, turned, before],
    )

    got1 = swap_core(grads1)
    grad_tokens, g_norm = call(
        kernel_d,
        "grad_tokens",
        [HB, HB, HB, HB, VM, HB],
        [((ROWS, D), F32, HB), ((1, D), F32, VM)],
        [
            pltpu.VMEM((ROWS, WIDE1), BF16),
            pltpu.VMEM((D, WIDE1), BF16),
            pltpu.VMEM((ROWS, D), F32),
            pltpu.VMEM((ROWS, D), BF16),
            pltpu.VMEM((ROWS, D), BF16),
            pltpu.VMEM((ROWS, D), F32),
            pltpu.VMEM((ROWS, D), F32),
            dma((5,)),
            dma((2,)),
        ],
        [d_proj, w1, d_hid, tokens, params, cotangent],
        8,
    )
    sum1 = call(
        kernel_g,
        "grad_conv_columns",
        [SM, VM, HB] + [VM] * 8 + [HB],
        [((208, HALF1), BF16, HB)] * 4,
        [
            pltpu.VMEM((4, 208, HALF1), BF16),
            pltpu.VMEM((ROWS, HALF1), BF16),
            pltpu.VMEM((16, HALF1), F32),
            dma,
            dma((4,)),
        ],
        [pos, turned, d_proj, got1, g_conv_w, g_conv_b, g_gated, g_norm]
        + [g_dt, g_alog, g_skip, sum2],
    )

    def ring(blocks, last):
        return [blocks[0]] + [
            lax.ppermute(blocks[r], "fsdp", ring_pairs(r, last)) for r in (1, 2, 3)
        ]

    sum1 = call(
        kernel_k, "ring_sums", [VM] * 4, [((64, HALF1), BF16, VM)] * 4, [], ring(sum1, True)
    )
    sum2 = jnp.sum(sum2.astype(F32), axis=0)
    as_gate = jnp.concatenate([sum2[:48], sum2[48:]], axis=1)
    sum2 = jnp.where(core == 0, as_gate, sum2.reshape(48, DI)).astype(BF16).reshape(8, 6, DI)
    sum2 = jnp.pad(sum2, ((0, 0), (0, 2), (0, 0))).reshape(64, DI)

    (both,) = call(
        kernel_l,
        "pieces_of_eight",
        [VM] * 5,
        [((64, DI + 3 * HALF1), BF16, VM)],
        [],
        ring(sum1, False) + [sum2],
    )
    both = lax.all_to_all(
        both.reshape(8, 8, DI + 3 * HALF1), "fsdp", 0, 0, axis_index_groups=EIGHTS
    ).reshape(64, DI + 3 * HALF1)
    return (out, grad_tokens) + tuple(
        call(
            kernel_h,
            "last_sums",
            [VM],
            [
                ((6 * NCOL,), F32, VM),
                ((6 * DI,), F32, VM),
                ((D,), F32, VM),
                ((CONV, CONV_CH), F32, VM),
                ((CONV_CH,), F32, VM),
                ((NH,), F32, VM),
                ((NH,), F32, VM),
                ((NH,), F32, VM),
                ((DI,), F32, VM),
            ],
            [pltpu.VMEM((8, DI + 2 * HALF1), F32)],
            [both],
        )
    )


def solution(mesh):
    rows = P("fsdp", None)
    flat = P("fsdp")
    same = P()
    return jax.shard_map(
        per_device,
        mesh=mesh,
        in_specs=(rows, flat, flat) + (same,) * 7 + (rows,),
        out_specs=(rows, rows, flat, flat) + (same,) * 7,
        check_vma=False,
    )
```

time: 259 us -> 204 us (0.79)
  starting transfers between devices: 70.7 us -> 32.4 us
  blocking collectives: 0 us -> 18 us
  local copies, waits for them, and re-layouts: 22.2 us -> 7.51 us
  other arithmetic: 12.7 us -> 3.8 us
  Pallas kernels: 101 us -> 92.6 us
    all_to_all x0 -> x1, blocking collectives: none -> 18 us  [per_device(): lax.all_to_all(both.reshape(8, 8, DI + 3 * HALF1), 'fsdp', 0, 0, axis_ind...]
    ppermute x10, starting transfers between devices: 24 us -> 7.71 us  [swap_core(): return lax.ppermute(value, 'fsdp', CORE_PAIRS)]
    ppermute x12 -> x6, waiting for transfers between devices: 26.2 us -> 14.5 us  [ring(): lax.ppermute(blocks[r], 'fsdp', ring_pairs(r, last))]
    pallas_call x4 -> x11, Pallas kernels: 101 us -> 92.6 us  [call(): pl.pallas_call(body, name=name, in_specs=[HB if spec is VM else spec for...]
    ppermute x12 -> x9, waiting for transfers between devices: 11.1 us -> 19.5 us  [ring_gather(): lax.ppermute(value, 'fsdp', ring_pairs(shift, last))]
    all_to_all x2 -> x1, starting transfers between devices: 12.9 us -> 4.47 us  [per_device(): sum2 = lax.all_to_all(sum2, 'fsdp', 0, 0, axis_index_groups=SIXTEENS)]
    add x3 -> x0, other arithmetic: 7.67 us -> none  [the longest x1 5.27 us: per_device(): sum2 = grads2[0].astype(F32) + swap_core(grads2[1]).astype(F32)]
    slice x15 -> x13, local copies, waits for them, and re-layouts: 7.3 us -> 0.13 us  [the longest x4 0.05 us: second_part(): as_gate = jnp.concatenate([v[:, HALF1:HALF1 + D], v[:, HALF1 + D:]], axis=0)]
  transfers between devices with their start and end apart: 37 -> 27, of which waited for: 16 -> 16; matrix products, arithmetic and copies ran while one was open for 8% -> 4% of each run, Pallas kernels for 15% -> 28%
where the time goes in v2:
time: 204 us; the launch traced here: 203 us
  Pallas kernels  92.6 us (45%)
  waiting for transfers between devices  47.3 us (23%)
  starting transfers between devices  32.4 us (16%)
  blocking collectives  18 us (9%)
  local copies, waits for them, and re-layouts  7.51 us (4%)
  other arithmetic  3.8 us (2%)
    pallas_call x11, Pallas kernels, call(): pl.pallas_call(body, name=name, in_specs=[HB if spec is VM else spec for...  92.6 us
    ppermute x9, waiting for transfers between devices, ring_gather(): lax.ppermute(value, 'fsdp', ring_pairs(shift, last))  19.5 us
    all_to_all x1, blocking collectives, per_device(): lax.all_to_all(both.reshape(8, 8, DI + 3 * HALF1), 'fsdp', 0, 0, axis_ind...  18 us
    ppermute x6, waiting for transfers between devices, ring(): lax.ppermute(blocks[r], 'fsdp', ring_pairs(r, last))  14.5 us
    ppermute x9, starting transfers between devices, ring_gather(): lax.ppermute(value, 'fsdp', ring_pairs(shift, last))  8.75 us
    ppermute x10, starting transfers between devices, swap_core(): return lax.ppermute(value, 'fsdp', CORE_PAIRS)  7.71 us
    ppermute x10, waiting for transfers between devices, swap_core(): return lax.ppermute(value, 'fsdp', CORE_PAIRS)  6.04 us
    all_to_all x1, starting transfers between devices, per_device(): eight = lax.all_to_all(sent, 'fsdp', 0, 0, axis_index_groups=EIGHTS)  5.97 us
  transfers between devices with their start and end apart: 27, of which 16 were waited for; matrix products, arithmetic and copies ran while one was open for 4% of the time, Pallas kernels for 28%

profile of v2, /device:TPU:1, one launch (start us, length us, event | category | flops | bytes accessed | tf_op | source)
XLA Modules:
  0.0 203.0 jit_solution(12077832530523776240)
XLA Ops:
  3.3 6.0 %all-to-all-start = ((bf16[8,6,2560]{2,1,0:T(8,128)(2,1)}), bf16[8,6,2560]{2,1,0:T(8,128)(2,1)S(1)}, u32[]{:S(2)}, u32[]{:S(2)}) async-start(bf16[8,6,2560]{2,1,0:T(8,128)(2,1)} %bitcast.2), calls=%async_computation | async-start | bytes 655360 | tf_op jit(solution)/shard_map/all_to_all | solution.py:916
  11.6 4.8 %all-to-all-done = bf16[8,6,2560]{2,1,0:T(8,128)(2,1)S(1)} async-done(((bf16[8,6,2560]{2,1,0:T(8,128)(2,1)}), bf16[8,6,2560]{2,1,0:T(8,128)(2,1)S(1)}, u32[]{:S(2)}, u32[]{:S(2)}) %all-to-all-start) | async-done | bytes 245792 | tf_op jit(solution)/shard_map/all_to_all | solution.py:916
  16.5 3.8 %collective-permute-start.2 = (bf16[48,2560]{1,0:T(8,128)(2,1)S(1)}, bf16[48,2560]{1,0:T(8,128)(2,1)S(1)}, u32[]{:S(2)}, u32[]{:S(2)}) collective-permute-start(bf16[48,2560]{1,0:T(8,128)(2,1)S(1)} %reshape.70), channel_id=1, source_target_pairs={{0,24},{1,97},{2,26},{3,99},{4,28},{5,101},{6,30},{7,103},{8,0},{9... | collective-permute-start | bytes 737288 | tf_op jit(solution)/shard_map/ppermute | solution.py:61
  21.1 4.9 %collective-permute-done.2 = bf16[48,2560]{1,0:T(8,128)(2,1)S(1)} collective-permute-done((bf16[48,2560]{1,0:T(8,128)(2,1)S(1)}, bf16[48,2560]{1,0:T(8,128)(2,1)S(1)}, u32[]{:S(2)}, u32[]{:S(2)}) %collective-permute-start.2) | collective-permute-done | bytes 245792 | tf_op jit(solution)/shard_map/ppermute | solution.py:61
  27.2 2.3 %collective-permute-done = bf16[48,2560]{1,0:T(8,128)(2,1)S(1)} collective-permute-done((bf16[48,2560]{1,0:T(8,128)(2,1)S(1)}, bf16[48,2560]{1,0:T(8,128)(2,1)S(1)}, u32[]{:S(2)}, u32[]{:S(2)}) %collective-permute-start) | collective-permute-done | bytes 245792 | tf_op jit(solution)/shard_map/ppermute | solution.py:61
  33.4 7.3 %collective-permute-done.5.refs_6_ = bf16[192,1024]{1,0:T(8,128)(2,1)S(1)} collective-permute-done((bf16[192,1024]{1,0:T(8,128)(2,1)S(1)}, bf16[192,1024]{1,0:T(8,128)(2,1)S(1)}, u32[]{:S(2)}, u32[]{:S(2)}) %collective-permute-start.5) | collective-permute-done | bytes 393248 | tf_op jit(solution)/shard_map/ppermute | solution.py:61
  40.7 3.7 %collective-permute-done.3.refs_4_ = bf16[192,1024]{1,0:T(8,128)(2,1)S(1)} collective-permute-done((bf16[192,1024]{1,0:T(8,128)(2,1)S(1)}, bf16[192,1024]{1,0:T(8,128)(2,1)S(1)}, u32[]{:S(2)}, u32[]{:S(2)}) %collective-permute-start.3) | collective-permute-done | bytes 393248 | tf_op jit(solution)/shard_map/ppermute | solution.py:61
  44.4 3.7 %collective-permute-start.6 = (bf16[192,1024]{1,0:T(8,128)(2,1)S(1)}, bf16[192,1024]{1,0:T(8,128)(2,1)S(1)}, u32[]{:S(2)}, u32[]{:S(2)}) collective-permute-start(bf16[192,1024]{1,0:T(8,128)(2,1)S(1)} %pad_maximum_fusion.1.refs_3_), channel_id=1, source_target_pairs={{0,1},{1,0},{2,3},{3,2},{4,5},{5,4},{6,7},{7,6},{8,9},{9,8},{10,11... | collective-permute-start | bytes 1179656 | tf_op jit(solution)/shard_map/ppermute | solution.py:66
  51.9 14.2 %forward_conv.1 = (bf16[512,768]{1,0:T(8,128)(2,1)}, bf16[768,512]{1,0:T(8,128)(2,1)}, bf16[768,2048]{1,0:T(8,128)(2,1)}, f32[2,264,1792]{2,1,0:T(8,128)}, f32[5...) custom-call(s32[3]{0:T(128)} %pad_add_fusion.refs_0_, ...), custom_call_target="tpu_custom_call" | custom-call | flops 15399999488 | bytes 100000 | tf_op jit(solution)/shard_map/forward_conv/pallas_call | solution.py:876
  68.6 8.2 %forward_ssd.1.refs_3_.refs_6_ = f32[512,1536]{1,0:T(8,128)} custom-call(f32[16,1792]{1,0:T(8,128)} %concatenate.37.refs_2_.refs_0_.refs_6_.refs_7_.refs_5_.refs_4_, bf16[512,1536]{1,0:T(8,128)(2,1)} %get-tuple-element.73.refs_1_.refs_0_, bf16[512,256]{1,0:T(8,128)(2,1)} %get-tuple-element.74.refs_2_.refs_1_, f32[512,128]{1,0:T(8,128)} %get-tuple-element.75.refs_3_.refs_2_, ...), custom_call_target="tpu_custom_call" | custom-call | flops 9900000256 | bytes 100000 | tf_op jit(solution)/shard_map/forward_ssd/pallas_call | solution.py:876
  76.9 18.8 %gate_output.1 = (bf16[512,768]{1,0:T(8,128)(2,1)}, f32[512,1536]{1,0:T(8,128)}, bf16[16,96,768]{2,1,0:T(8,128)(2,1)}, f32[512,768]{1,0:T(8,128)}, bf16[512,1536...) custom-call(s32[3]{0:T(128)} %pad_add_fusion.refs_0_, bf16[512,768]{1,0:T(8,128)(2,1)} %get-tuple-element.71.refs_1_, ...), custom_call_target="tpu_custom_call" | custom-call | flops 19800000512 | bytes 100000 | tf_op jit(solution)/shard_map/gate_output/pallas_call | solution.py:876
  95.7 4.9 %collective-permute-done.17.refs_5_ = bf16[16,96,768]{2,1,0:T(8,128)(2,1)} collective-permute-done((bf16[16,96,768]{2,1,0:T(8,128)(2,1)}, bf16[16,96,768]{2,1,0:T(8,128)(2,1)}, u32[]{:S(2)}, u32[]{:S(2)}) %collective-permute-start.17) | collective-permute-done | bytes 2359328 | tf_op jit(solution)/shard_map/ppermute | solution.py:66
  100.6 5.9 %grad_gate_out.1.refs_7_ = bf16[16,96,768]{2,1,0:T(8,128)(2,1)} custom-call(s32[3]{0:T(128)} %pad_add_fusion.refs_0_, bf16[768,512]{1,0:T(8,128)(2,1)} %get-tuple-element.72.refs_2_.refs_1_.refs_6_, bf16[512,768]{1,0:T(8,128)(2,1)} %refs_5_.3, bf16[512,1536]{1,0:T(8,128)(2,1)} %get-tuple-element.85.refs_3_, bf16[512,1536]{1,0:T(8,128)(2,1)} %get-tuple-element.86.refs_4_, ...), custom_call_target="tpu_custom_call" | custom-call | flops 11000000 | bytes 100000 | tf_op jit(solution)/shard_map/grad_gate_out/pallas_call | solution.py:876
  106.5 4.5 %all-to-all-start.1 = ((bf16[16,96,768]{2,1,0:T(8,128)(2,1)}), bf16[16,96,768]{2,1,0:T(8,128)(2,1)}, u32[]{:S(2)}, u32[]{:S(2)}) async-start(bf16[16,96,768]{2,1,0:T(8,128)(2,1)} %grad_gate_out.1.refs_7_), calls=%async_computation.1 | async-start | bytes 4718592 | tf_op jit(solution)/shard_map/all_to_all | solution.py:1070
  111.0 13.8 %backward_ssd.1 = (f32[512,1792]{1,0:T(8,128)}, bf16[512,128]{1,0:T(8,128)(2,1)}, f32[1,128]{1,0:T(1,128)}, f32[1,128]{1,0:T(1,128)}, f32[1,128]{1,0:T(1,128)}) custom-call(bf16[512,1536]{1,0:T(8,128)(2,1)} %get-tuple-element.73.refs_1_.refs_0_, bf16[512,256]{1,0:T(8,128)(2,1)} %get-tuple-element.74.refs_2_.refs_1_, ...), custom_call_target="tpu_custom_call" | custom-call | flops 15399999488 | bytes 100000 | tf_op jit(solution)/shard_map/backward_ssd/pallas_call | solution.py:876
  124.8 12.4 %backward_conv.1 = (bf16[768,1024]{1,0:T(8,128)(2,1)}, bf16[512,2048]{1,0:T(8,128)(2,1)}, f32[4,1792]{1,0:T(4,128)}, f32[1,1792]{1,0:T(1,128)}) custom-call(s32[3]{0:T(128)} %pad_add_fusion.refs_0_, f32[512,1792]{1,0:T(8,128)} %get-tuple-element.81.refs_1_, bf16[512,128]{1,0:T(8,128)(2,1)} %get-tuple-element.82.refs_2_, ...), custom_call_target="tpu_custom_call" | custom-call | flops 11000000 | bytes 100000 | tf_op jit(solution)/shard_map/backward_conv/pallas_call | solution.py:876
  138.0 7.2 %grad_tokens.1 = (f32[512,768]{1,0:T(8,128)}, f32[1,768]{1,0:T(1,128)}) custom-call(bf16[512,2048]{1,0:T(8,128)(2,1)} %get-tuple-element.88.refs_0_.refs_2_, bf16[768,2048]{1,0:T(8,128)(2,1)} %get-tuple-element.89.refs_1_, f32[512,768]{1,0:T(8,128)} %get-tuple-element.90.refs_2_, bf16[512,768]{1,0:T(8,128)(2,1)} %refs_3_.1, ...), custom_call_target="tpu_custom_call" | custom-call | flops 8800000000 | bytes 100000 | tf_op jit(solution)/shard_map/grad_tokens/pallas_call | solution.py:876
  145.2 2.4 %all-to-all-done.1.refs_11_ = bf16[16,96,768]{2,1,0:T(8,128)(2,1)} async-done(((bf16[16,96,768]{2,1,0:T(8,128)(2,1)}), bf16[16,96,768]{2,1,0:T(8,128)(2,1)}, u32[]{:S(2)}, u32[]{:S(2)}) %all-to-all-start.1) | async-done | bytes 2359328 | tf_op jit(solution)/shard_map/all_to_all | solution.py:1070
  150.3 5.6 %grad_conv_columns.1 = (bf16[208,1024]{1,0:T(8,128)(2,1)}, bf16[208,1024]{1,0:T(8,128)(2,1)}, bf16[208,1024]{1,0:T(8,128)(2,1)}, bf16[208,1024]{1,0:T(8,128)(2,1)}) custom-call(s32[3]{0:T(128)} %pad_add_fusion.refs_0_, bf16[768,512]{1,0:T(8,128)(2,1)} %get-tuple-element.72.refs_2_.refs_1_.refs_6_, bf16[512,2048]{1,0:T(8,128)(2,1)} %get-tuple-element.88.refs_0_.refs_2_, ...), custom_call_target="tpu_custom_call" | custom-call | flops 11000000 | bytes 100000 | tf_op jit(solution)/shard_map/grad_conv_columns/pallas_call | solution.py:876
  159.7 9.7 %collective-permute-done.19.refs_1_ = bf16[208,1024]{1,0:T(8,128)(2,1)S(1)} collective-permute-done((bf16[208,1024]{1,0:T(8,128)(2,1)}, bf16[208,1024]{1,0:T(8,128)(2,1)S(1)}, u32[]{:S(2)}, u32[]{:S(2)}) %collective-permute-start.19) | collective-permute-done | bytes 426016 | tf_op jit(solution)/shard_map/ppermute | solution.py:1133
  170.1 2.3 %ring_sums.1 = (bf16[64,1024]{1,0:T(8,128)(2,1)}, bf16[64,1024]{1,0:T(8,128)(2,1)}, bf16[64,1024]{1,0:T(8,128)(2,1)}, bf16[64,1024]{1,0:T(8,128)(2,1)}) custom-call(bf16[208,1024]{1,0:T(8,128)(2,1)} %get-tuple-element.100.refs_0_, bf16[208,1024]{1,0:T(8,128)(2,1)} %copy-done.1, bf16[208,1024]{1,0:T(8,128)(2,1)} %collective-permute-done.20.refs_2_, ...), custom_call_target="tpu_custom_call" | custom-call | flops 11000000 | bytes 100000 | tf_op jit(solution)/shard_map/ring_sums/pallas_call | solution.py:876
  172.5 2.4 %collective-permute-start.23 = (bf16[64,1024]{1,0:T(8,128)(2,1)}, bf16[64,1024]{1,0:T(8,128)(2,1)S(1)}, u32[]{:S(2)}, u32[]{:S(2)}) collective-permute-start(bf16[64,1024]{1,0:T(8,128)(2,1)} %get-tuple-element.106), channel_id=1, source_target_pairs={{0,16},{1,65},{2,18},{3,67},{4,20},{5,69},{6,22},{7,71},{8,24},{9,... | collective-permute-start | bytes 393224 | tf_op jit(solution)/shard_map/ppermute | solution.py:1133
  175.9 3.5 %collective-permute-done.22.refs_1_ = bf16[64,1024]{1,0:T(8,128)(2,1)S(1)} collective-permute-done((bf16[64,1024]{1,0:T(8,128)(2,1)}, bf16[64,1024]{1,0:T(8,128)(2,1)S(1)}, u32[]{:S(2)}, u32[]{:S(2)}) %collective-permute-start.22) | collective-permute-done | bytes 131104 | tf_op jit(solution)/shard_map/ppermute | solution.py:1133
  182.9 18.0 %all_to_all.15 = bf16[8,8,4608]{2,1,0:T(8,128)(2,1)} all-to-all(bf16[8,8,4608]{2,1,0:T(8,128)(2,1)} %bitcast.13), channel_id=1, replica_groups={{0,1,2,3,4,5,6,7},{8,9,10,11,12,13,14,15},{16,17,18,19,20,21,22,23},{24..., dimensions={0} | all-to-all | bytes 1179648 | tf_op jit(solution)/shard_map/all_to_all | solution.py:1152
  (136 shorter events, 31.2 us)
Async XLA Ops:
  3.3 13.1 %all-to-all-start = ((bf16[8,6,2560]{2,1,0:T(8,128)(2,1)}), bf16[8,6,2560]{2,1,0:T(8,128)(2,1)S(1)}, u32[]{:S(2)}, u32[]{:S(2)}) async-start(bf16[8,6,2560]{2,1,0:T(8,128)(2,1)} %bitcast.2), calls=%async_computation | async-start | bytes 655360 | tf_op jit(solution)/shard_map/all_to_all | solution.py:916
  16.5 9.6 %collective-permute-start.2 = (bf16[48,2560]{1,0:T(8,128)(2,1)S(1)}, bf16[48,2560]{1,0:T(8,128)(2,1)S(1)}, u32[]{:S(2)}, u32[]{:S(2)}) collective-permute-start(bf16[48,2560]{1,0:T(8,128)(2,1)S(1)} %reshape.70), channel_id=1, source_target_pairs={{0,24},{1,97},{2,26},{3,99},{4,28},{5,101},{6,30},{7,103},{8,0},{9... | collective-permute-start | bytes 737288 | tf_op jit(solution)/shard_map/ppermute | solution.py:61
  20.3 6.9 %collective-permute-start.1 = (bf16[48,2560]{1,0:T(8,128)(2,1)S(1)}, bf16[48,2560]{1,0:T(8,128)(2,1)S(1)}, u32[]{:S(2)}, u32[]{:S(2)}) collective-permute-start(bf16[48,2560]{1,0:T(8,128)(2,1)S(1)} %reshape.70), channel_id=1, source_target_pairs={{0,16},{1,65},{2,18},{3,67},{4,20},{5,69},{6,22},{7,71},{8,24},{9,... | collective-permute-start | bytes 737288 | tf_op jit(solution)/shard_map/ppermute | solution.py:61
  20.3 9.2 %collective-permute-start = (bf16[48,2560]{1,0:T(8,128)(2,1)S(1)}, bf16[48,2560]{1,0:T(8,128)(2,1)S(1)}, u32[]{:S(2)}, u32[]{:S(2)}) collective-permute-start(bf16[48,2560]{1,0:T(8,128)(2,1)S(1)} %reshape.70), channel_id=1, source_target_pairs={{0,8},{1,33},{2,10},{3,35},{4,12},{5,37},{6,14},{7,39},{8,16},{9,4... | collective-permute-start | bytes 737288 | tf_op jit(solution)/shard_map/ppermute | solution.py:61
  29.5 11.2 %collective-permute-start.5 = (bf16[192,1024]{1,0:T(8,128)(2,1)S(1)}, bf16[192,1024]{1,0:T(8,128)(2,1)S(1)}, u32[]{:S(2)}, u32[]{:S(2)}) collective-permute-start(bf16[192,1024]{1,0:T(8,128)(2,1)S(1)} %pad_maximum_fusion.1.refs_3_), channel_id=1, source_target_pairs={{0,96},{1,25},{2,98},{3,27},{4,100},{5,29},{6,102},{7,31},{8,104},... | collective-permute-start | bytes 1179656 | tf_op jit(solution)/shard_map/ppermute | solution.py:61
  31.8 8.9 %collective-permute-start.4 = (bf16[192,1024]{1,0:T(8,128)(2,1)S(1)}, bf16[192,1024]{1,0:T(8,128)(2,1)S(1)}, u32[]{:S(2)}, u32[]{:S(2)}) collective-permute-start(bf16[192,1024]{1,0:T(8,128)(2,1)S(1)} %pad_maximum_fusion.1.refs_3_), channel_id=1, source_target_pairs={{0,64},{1,17},{2,66},{3,19},{4,68},{5,21},{6,70},{7,23},{8,72},{9,... | collective-permute-start | bytes 1179656 | tf_op jit(solution)/shard_map/ppermute | solution.py:61
  32.3 12.1 %collective-permute-start.3 = (bf16[192,1024]{1,0:T(8,128)(2,1)S(1)}, bf16[192,1024]{1,0:T(8,128)(2,1)S(1)}, u32[]{:S(2)}, u32[]{:S(2)}) collective-permute-start(bf16[192,1024]{1,0:T(8,128)(2,1)S(1)} %pad_maximum_fusion.1.refs_3_), channel_id=1, source_target_pairs={{0,32},{1,9},{2,34},{3,11},{4,36},{5,13},{6,38},{7,15},{8,40},{9,1... | collective-permute-start | bytes 1179656 | tf_op jit(solution)/shard_map/ppermute | solution.py:61
  44.4 5.0 %collective-permute-start.6 = (bf16[192,1024]{1,0:T(8,128)(2,1)S(1)}, bf16[192,1024]{1,0:T(8,128)(2,1)S(1)}, u32[]{:S(2)}, u32[]{:S(2)}) collective-permute-start(bf16[192,1024]{1,0:T(8,128)(2,1)S(1)} %pad_maximum_fusion.1.refs_3_), channel_id=1, source_target_pairs={{0,1},{1,0},{2,3},{3,2},{4,5},{5,4},{6,7},{7,6},{8,9},{9,8},{10,11... | collective-permute-start | bytes 1179656 | tf_op jit(solution)/shard_map/ppermute | solution.py:66
  48.7 28.1 %collective-permute-start.13 = (bf16[384,768]{1,0:T(8,128)(2,1)S(1)}, bf16[384,768]{1,0:T(8,128)(2,1)}, u32[]{:S(2)}, u32[]{:S(2)}) collective-permute-start(bf16[384,768]{1,0:T(8,128)(2,1)S(1)} %pad_maximum_fusion.refs_7_), channel_id=1, source_target_pairs={{0,1},{1,0},{2,3},{3,2},{4,5},{5,4},{6,7},{7,6},{8,9},{9,8},{10,11... | collective-permute-start | bytes 1769480 | tf_op jit(solution)/shard_map/ppermute | solution.py:66
  49.5 16.7 %collective-permute-start.12 = (bf16[384,768]{1,0:T(8,128)(2,1)S(1)}, bf16[384,768]{1,0:T(8,128)(2,1)}, u32[]{:S(2)}, u32[]{:S(2)}) collective-permute-start(bf16[384,768]{1,0:T(8,128)(2,1)S(1)} %pad_maximum_fusion.refs_7_), channel_id=1, source_target_pairs={{0,96},{1,25},{2,98},{3,27},{4,100},{5,29},{6,102},{7,31},{8,104},... | collective-permute-start | bytes 1769480 | tf_op jit(solution)/shard_map/ppermute | solution.py:61
  50.0 16.6 %collective-permute-start.11 = (bf16[384,768]{1,0:T(8,128)(2,1)S(1)}, bf16[384,768]{1,0:T(8,128)(2,1)}, u32[]{:S(2)}, u32[]{:S(2)}) collective-permute-start(bf16[384,768]{1,0:T(8,128)(2,1)S(1)} %pad_maximum_fusion.refs_7_), channel_id=1, source_target_pairs={{0,64},{1,17},{2,66},{3,19},{4,68},{5,21},{6,70},{7,23},{8,72},{9,... | collective-permute-start | bytes 1769480 | tf_op jit(solution)/shard_map/ppermute | solution.py:61
  51.2 15.8 %collective-permute-start.10 = (bf16[384,768]{1,0:T(8,128)(2,1)S(1)}, bf16[384,768]{1,0:T(8,128)(2,1)}, u32[]{:S(2)}, u32[]{:S(2)}) collective-permute-start(bf16[384,768]{1,0:T(8,128)(2,1)S(1)} %pad_maximum_fusion.refs_7_), channel_id=1, source_target_pairs={{0,32},{1,9},{2,34},{3,11},{4,36},{5,13},{6,38},{7,15},{8,40},{9,1... | collective-permute-start | bytes 1769480 | tf_op jit(solution)/shard_map/ppermute | solution.py:61
  66.2 10.6 %collective-permute-start.16 = (bf16[384,768]{1,0:T(8,128)(2,1)}, bf16[384,768]{1,0:T(8,128)(2,1)}, u32[]{:S(2)}, u32[]{:S(2)}) collective-permute-start(bf16[384,768]{1,0:T(8,128)(2,1)} %collective-permute-done.12.refs_10_), channel_id=1, source_target_pairs={{0,1},{1,0},{2,3},{3,2},{4,5},{5,4},{6,7},{7,6},{8,9},{9,8},{10,11... | collective-permute-start | bytes 1769480 | tf_op jit(solution)/shard_map/ppermute | solution.py:66
  66.6 10.2 %collective-permute-start.15 = (bf16[384,768]{1,0:T(8,128)(2,1)}, bf16[384,768]{1,0:T(8,128)(2,1)}, u32[]{:S(2)}, u32[]{:S(2)}) collective-permute-start(bf16[384,768]{1,0:T(8,128)(2,1)} %collective-permute-done.11.refs_9_), channel_id=1, source_target_pairs={{0,1},{1,0},{2,3},{3,2},{4,5},{5,4},{6,7},{7,6},{8,9},{9,8},{10,11... | collective-permute-start | bytes 1769480 | tf_op jit(solution)/shard_map/ppermute | solution.py:66
  67.0 9.9 %collective-permute-start.14 = (bf16[384,768]{1,0:T(8,128)(2,1)}, bf16[384,768]{1,0:T(8,128)(2,1)}, u32[]{:S(2)}, u32[]{:S(2)}) collective-permute-start(bf16[384,768]{1,0:T(8,128)(2,1)} %collective-permute-done.10.refs_8_), channel_id=1, source_target_pairs={{0,1},{1,0},{2,3},{3,2},{4,5},{5,4},{6,7},{7,6},{8,9},{9,8},{10,11... | collective-permute-start | bytes 1769480 | tf_op jit(solution)/shard_map/ppermute | solution.py:66
  95.6 5.0 %collective-permute-start.17 = (bf16[16,96,768]{2,1,0:T(8,128)(2,1)}, bf16[16,96,768]{2,1,0:T(8,128)(2,1)}, u32[]{:S(2)}, u32[]{:S(2)}) collective-permute-start(bf16[16,96,768]{2,1,0:T(8,128)(2,1)} %get-tuple-element.87), channel_id=1, source_target_pairs={{0,1},{1,0},{2,3},{3,2},{4,5},{5,4},{6,7},{7,6},{8,9},{9,8},{10,11... | collective-permute-start | bytes 7077896 | tf_op jit(solution)/shard_map/ppermute | solution.py:66
  106.5 41.0 %all-to-all-start.1 = ((bf16[16,96,768]{2,1,0:T(8,128)(2,1)}), bf16[16,96,768]{2,1,0:T(8,128)(2,1)}, u32[]{:S(2)}, u32[]{:S(2)}) async-start(bf16[16,96,768]{2,1,0:T(8,128)(2,1)} %grad_gate_out.1.refs_7_), calls=%async_computation.1 | async-start | bytes 4718592 | tf_op jit(solution)/shard_map/all_to_all | solution.py:1070
  137.2 13.1 %collective-permute-start.18 = (bf16[768,1024]{1,0:T(8,128)(2,1)}, bf16[768,1024]{1,0:T(8,128)(2,1)}, u32[]{:S(2)}, u32[]{:S(2)}) collective-permute-start(bf16[768,1024]{1,0:T(8,128)(2,1)} %get-tuple-element.92), channel_id=1, source_target_pairs={{0,1},{1,0},{2,3},{3,2},{4,5},{5,4},{6,7},{7,6},{8,9},{9,8},{10,11... | collective-permute-start | bytes 4718600 | tf_op jit(solution)/shard_map/ppermute | solution.py:66
  155.9 13.4 %collective-permute-start.19 = (bf16[208,1024]{1,0:T(8,128)(2,1)}, bf16[208,1024]{1,0:T(8,128)(2,1)S(1)}, u32[]{:S(2)}, u32[]{:S(2)}) collective-permute-start(bf16[208,1024]{1,0:T(8,128)(2,1)} %get-tuple-element.101), channel_id=1, source_target_pairs={{0,32},{1,9},{2,34},{3,11},{4,36},{5,13},{6,38},{7,15},{8,40},{9,1... | collective-permute-start | bytes 1277960 | tf_op jit(solution)/shard_map/ppermute | solution.py:1133
  156.0 13.4 %collective-permute-start.20 = (bf16[208,1024]{1,0:T(8,128)(2,1)}, bf16[208,1024]{1,0:T(8,128)(2,1)}, u32[]{:S(2)}, u32[]{:S(2)}) collective-permute-start(bf16[208,1024]{1,0:T(8,128)(2,1)} %get-tuple-element.102), channel_id=1, source_target_pairs={{0,64},{1,17},{2,66},{3,19},{4,68},{5,21},{6,70},{7,23},{8,72},{9,... | collective-permute-start | bytes 1277960 | tf_op jit(solution)/shard_map/ppermute | solution.py:1133
  157.5 12.5 %collective-permute-start.21 = (bf16[208,1024]{1,0:T(8,128)(2,1)}, bf16[208,1024]{1,0:T(8,128)(2,1)}, u32[]{:S(2)}, u32[]{:S(2)}) collective-permute-start(bf16[208,1024]{1,0:T(8,128)(2,1)} %get-tuple-element.103), channel_id=1, source_target_pairs={{0,96},{1,25},{2,98},{3,27},{4,100},{5,29},{6,102},{7,31},{8,104},... | collective-permute-start | bytes 1277960 | tf_op jit(solution)/shard_map/ppermute | solution.py:1133
  172.5 7.0 %collective-permute-start.22 = (bf16[64,1024]{1,0:T(8,128)(2,1)}, bf16[64,1024]{1,0:T(8,128)(2,1)S(1)}, u32[]{:S(2)}, u32[]{:S(2)}) collective-permute-start(bf16[64,1024]{1,0:T(8,128)(2,1)} %get-tuple-element.105), channel_id=1, source_target_pairs={{0,8},{1,33},{2,10},{3,35},{4,12},{5,37},{6,14},{7,39},{8,16},{9,4... | collective-permute-start | bytes 393224 | tf_op jit(solution)/shard_map/ppermute | solution.py:1133
  172.5 6.9 %collective-permute-start.23 = (bf16[64,1024]{1,0:T(8,128)(2,1)}, bf16[64,1024]{1,0:T(8,128)(2,1)S(1)}, u32[]{:S(2)}, u32[]{:S(2)}) collective-permute-start(bf16[64,1024]{1,0:T(8,128)(2,1)} %get-tuple-element.106), channel_id=1, source_target_pairs={{0,16},{1,65},{2,18},{3,67},{4,20},{5,69},{6,22},{7,71},{8,24},{9,... | collective-permute-start | bytes 393224 | tf_op jit(solution)/shard_map/ppermute | solution.py:1133
  174.9 5.1 %collective-permute-start.24 = (bf16[64,1024]{1,0:T(8,128)(2,1)}, bf16[64,1024]{1,0:T(8,128)(2,1)S(1)}, u32[]{:S(2)}, u32[]{:S(2)}) collective-permute-start(bf16[64,1024]{1,0:T(8,128)(2,1)} %get-tuple-element.107), channel_id=1, source_target_pairs={{0,24},{1,97},{2,26},{3,99},{4,28},{5,101},{6,30},{7,103},{8,0},{9... | collective-permute-start | bytes 393224 | tf_op jit(solution)/shard_map/ppermute | solution.py:1133
  (22 other events, 151.0 us)
